TPU v7x, 128 devices: a whole 4x4x4 slice. The times are simulated.
128 devices in a mesh: dp: 8 (over x, z_hi), seq: 16 (over z_lo, y, core).
Axes of the slice: x: 4, y: 4, z: 4 (z_hi: 2, z_lo: 2; z = z_hi * 2 + z_lo), core: 2. Of those that a mesh axis runs over, the one named last changes fastest.
Arguments:
- grad_seq: bfloat16 [8, 4096, 8192], P('dp', 'seq'), may hold values from -6 to 6
- features: bfloat16 [8, 1024, 5120], P('dp', 'seq'), may hold values from -6 to 6
- merger_norm_gain: float32 [1280], replicated, may hold values from 0.25 to 1.75
- w_in: bfloat16 [5120, 3072], P(None, 'dp'), may hold values from -0.078125 to 0.078125
- b_in: float32 [3072], P('dp'), may hold values from -3 to 3
- w_out: bfloat16 [3072, 8192], P('dp'), may hold values from -0.0625 to 0.0625
- image_counts: int32 [8, 64], P('dp'), may hold values from 1 to 16, as said below
- sample_owner: int32 [8, 64], P('dp'), may hold values from 0 to 15, as said below
- image_starts: int32 [8, 64], P('dp'), may hold values from 0 to 4095, as said below
Outputs:
- merger_input_gradient: bfloat16 [8, 1024, 5120], P('dp', 'seq')
- grad_w1: bfloat16 [5120, 3072], P('seq', 'dp')
- grad_w2: bfloat16 [3072, 8192], P('dp', 'seq')
Inputs may be any that keep to these rules, and one draw needn't show every extreme that they name: `sample_owner`: in each group each owner has exactly 4 samples, no two of them in the same sequence shard. `image_counts`: in each group the counts of one owner's samples sum to at most 64, exactly 64 for some owner; the image tokens within one sequence shard of 256 tokens number at most 64, exactly 64 in some shard. `image_starts`: Samples' image tokens occupy disjoint ranges of the sequence in increasing sample order, each range inside one sequence shard of 256 tokens.
All inputs are finite; a program needn't handle non-finite values.
Results may differ from a plain program's by a relative error of at most 0.024.
Values may be sent and summed in bfloat16 or wider, within the bound.
A program may use at most 128 MiB of HBM per device.

v0:
```python
import jax
import jax.numpy as jnp
from jax import lax
from jax.sharding import PartitionSpec as P

EPS = 1e-06


def slot_positions(counts_row, owner_row, starts_row, owners, capacity):
    chosen = owner_row[None, :] == jnp.arange(owners, dtype=jnp.int32)[:, None]
    taken = jnp.where(chosen, counts_row[None, :], 0)
    before = jnp.cumsum(taken, axis=1) - taken
    slots = jnp.arange(capacity, dtype=jnp.int32)
    inside = (
        chosen[:, None, :]
        & (slots[None, :, None] >= before[:, None, :])
        & (slots[None, :, None] < (before + taken)[:, None, :])
    )
    located = jnp.where(
        inside, starts_row[None, None, :] + slots[None, :, None] - before[:, None, :], 0
    )
    return jnp.where(jnp.any(inside, axis=2), jnp.sum(located, axis=2), -1)


def normal_cdf(value):
    return 0.5 * (1.0 + jax.scipy.special.erf(value * 0.7071067811865476))


def normal_pdf(value):
    return jnp.exp(-0.5 * value * value) * 0.3989422804014327


def layer_normalize(rows, gain_vector):
    feature_count = rows.shape[0]
    vectors = rows.astype(jnp.float32).reshape(feature_count, 4, -1)
    subtract_mean = vectors - jnp.mean(vectors, axis=2, keepdims=True)
    inverse_deviation = lax.rsqrt(
        jnp.mean(subtract_mean * subtract_mean, axis=2, keepdims=True) + EPS
    )
    standardized_input = subtract_mean * inverse_deviation
    normalized_rows = (
        (standardized_input * gain_vector).reshape(feature_count, -1).astype(jnp.bfloat16)
    )
    return (normalized_rows, standardized_input, inverse_deviation)


def apply_norm_gain(normalized_gradient, standardized_input, inverse_deviation, gain_vector):
    feature_count = normalized_gradient.shape[0]
    gain_scaled = normalized_gradient.reshape(feature_count, 4, -1) * gain_vector
    mean_removed = (
        gain_scaled
        - jnp.mean(gain_scaled, axis=2, keepdims=True)
        - standardized_input * jnp.mean(gain_scaled * standardized_input, axis=2, keepdims=True)
    )
    return (mean_removed * inverse_deviation).reshape(feature_count, -1)


def return_gradients(local_rows, positions, counts_row, starts_row, seq_index):
    owners, capacity = positions.shape
    tok_dev = local_rows.shape[0]
    base_row = seq_index * tok_dev
    wanted = lax.dynamic_index_in_dim(positions, seq_index, 0, False)
    wanted_valid = wanted >= 0
    shard_of = starts_row // tok_dev
    packing = slot_positions(counts_row, shard_of, starts_row, owners, capacity)
    mine = lax.dynamic_index_in_dim(packing, seq_index, 0, False)
    offset_rows = jnp.clip(mine - base_row, 0, tok_dev - 1)
    packed = jnp.where(
        (mine >= 0)[:, None], jnp.take(local_rows, offset_rows, axis=0), jnp.zeros((), jnp.bfloat16)
    )
    everything = lax.all_gather(packed, "seq", axis=0, tiled=True)
    flat_packing = packing.reshape(-1)
    matched = (wanted[:, None] == flat_packing[None, :]) & wanted_valid[:, None]
    index = jnp.sum(
        jnp.where(matched, jnp.arange(owners * capacity, dtype=jnp.int32)[None, :], 0), axis=1
    )
    returned = jnp.where(
        jnp.any(matched, axis=1)[:, None],
        jnp.take(everything, index, axis=0),
        jnp.zeros((), jnp.bfloat16),
    )
    return returned


def gather_normed(normalized_rows):
    return lax.all_gather(normalized_rows, "dp", axis=0, tiled=True)


def local(
    grad_seq,
    features,
    merger_norm_gain,
    w_in,
    b_in,
    w_out,
    image_counts,
    sample_owner,
    image_starts,
):
    owners = lax.axis_size("seq")
    seq_index = lax.axis_index("seq")
    capacity = features.shape[1]
    positions = slot_positions(image_counts[0], sample_owner[0], image_starts[0], owners, capacity)
    normalized_rows, standardized_input, inverse_deviation = layer_normalize(
        features[0], merger_norm_gain
    )
    returned = return_gradients(grad_seq[0], positions, image_counts[0], image_starts[0], seq_index)
    normed_all = gather_normed(normalized_rows)
    pre_all = jnp.dot(normed_all, w_in, preferred_element_type=jnp.float32) + b_in
    activated_all = (pre_all * normal_cdf(pre_all)).astype(jnp.bfloat16)
    slope_all = normal_cdf(pre_all) + pre_all * normal_pdf(pre_all)
    piece = lax.all_gather(returned, "dp", axis=0, tiled=True)
    grad_hidden = lax.dot_general(
        piece, w_out, (((1,), (1,)), ((), ())), preferred_element_type=jnp.float32
    )
    grad_pre = (grad_hidden * slope_all).astype(jnp.bfloat16)
    weight_total = lax.dot_general(
        activated_all, piece, (((0,), (0,)), ((), ())), preferred_element_type=jnp.float32
    )
    block = grad_pre
    normalized_gradient = lax.psum_scatter(
        lax.dot_general(
            block, w_in, (((1,), (1,)), ((), ())), preferred_element_type=jnp.float32
        ).astype(jnp.bfloat16),
        "dp",
        scatter_dimension=0,
        tiled=True,
    ).astype(jnp.float32)
    merger_input_gradient = apply_norm_gain(
        normalized_gradient, standardized_input, inverse_deviation, merger_norm_gain
    ).astype(jnp.bfloat16)
    block = normed_all
    grad_w1 = lax.psum_scatter(
        lax.dot_general(
            block, grad_pre, (((0,), (0,)), ((), ())), preferred_element_type=jnp.float32
        ).astype(jnp.bfloat16),
        "seq",
        scatter_dimension=0,
        tiled=True,
    )
    grad_w2 = lax.psum_scatter(
        weight_total.astype(jnp.bfloat16), "seq", scatter_dimension=1, tiled=True
    )
    return (merger_input_gradient[None], grad_w1, grad_w2)


def solution(mesh):
    in_specs = (
        P("dp", "seq", None),
        P("dp", "seq", None),
        P(),
        P(None, "dp"),
        P("dp"),
        P("dp", None),
        P("dp", None),
        P("dp", None),
        P("dp", None),
    )
    out_specs = (P("dp", "seq", None), P("seq", "dp"), P("dp", "seq"))
    return jax.shard_map(local, mesh=mesh, in_specs=in_specs, out_specs=out_specs, check_vma=False)
```

profile of v0, /device:TPU:1, one launch (start us, length us, event | category | flops | bytes accessed | tf_op | source)
XLA Modules:
  0.0 554.9 jit_solution(1796336761692675833)
XLA Ops:
  7.2 0.0 all-gather.4.cloned.1.call-start
  7.2 0.7 fusion.18
  7.9 0.7 iota_compare_fusion.5
  8.6 0.7 broadcast_select_fusion.2
  9.2 0.2 reduce_window_sum.17
  9.4 0.2 reduce_window_sum.18
  9.7 0.7 iota_add_fusion
  10.3 0.7 fusion.14
  11.0 0.4 fusion.11
  11.4 0.4 fusion.12
  11.7 0.6 select_reduce_fusion.1
  12.5 4.9 gather_fusion
  17.3 0.0 copy-start.1
  17.4 1.2 select_select_fusion.1
  18.6 0.0 all-gather.4.cloned.1.call-update
  18.6 0.0 all-gather.8.cloned.1.call-start
  18.6 0.0 copy-done.1
  18.6 0.6 reshape.264
  19.3 0.2 reduce_sum.69
  19.5 0.5 multiply_reduce_fusion.1
  20.0 0.2 mul.103
  20.3 0.2 copy.13
  20.5 0.2 sub.98
  20.8 0.0 copy-start.3
  20.8 1.3 copy.12
  22.1 0.0 copy-done.3
  22.1 2.3 multiply_convert_fusion.1
  24.4 0.0 all-gather.8.cloned.1.call-update
  24.5 0.0 all-gather.6.cloned.1.call-start
  24.5 0.1 select_n.104
  24.6 0.2 select_reduce_fusion.2
  24.8 0.2 fusion.13
  25.0 89.0 %all-gather.4.cloned.1.call-done = bf16[1024,8192]{1,0:T(8,128)(2,1)} async-done(((bf16[64,8192]{1,0:T(8,128)(2,1)}), bf16[1024,8192]{1,0:T(8,128)(2,1)}) %all-gather.4.cloned.1.call-update) | async-done | bytes 16777232 | tf_op jit(solution)/shard_map/all_gather | solution.py:71
  114.0 11.1 %gather_fusion.1 = bf16[64,8192]{1,0:T(8,128)(2,1)} fusion(bf16[1024,8192]{1,0:T(8,128)(2,1)} %all-gather.4.cloned.1.call-done, s32[1024]{0:T(1024)S(1)} %pad_clamp_fusion), kind=kCustom, calls=%fused_computation.1 | custom fusion | bytes 2097408 | tf_op jit(solution)/shard_map/jit(_take)/gather | solution.py:79
  125.1 2.4 select_select_fusion
  127.5 0.0 all-gather.6.cloned.1.call-update
  127.6 0.2 reduce-scatter.4.cloned.1.call-start
  127.8 69.4 %all-gather.8.cloned.1.call-done = bf16[512,5120]{1,0:T(8,128)(2,1)} async-done(((bf16[64,5120]{1,0:T(8,128)(2,1)}), bf16[512,5120]{1,0:T(8,128)(2,1)}) %all-gather.8.cloned.1.call-update) | async-done | bytes 5242896 | tf_op jit(solution)/shard_map/all_gather | solution.py:86
  197.1 0.0 copy-done.5
  197.1 7.5 %convolution_add_fusion = f32[512,384]{1,0:T(8,128)} fusion(bf16[512,5120]{1,0:T(8,128)(2,1)} %all-gather.8.cloned.1.call-done, bf16[5120,384]{1,0:T(8,128)(2,1)} %param.12, f32[384]{0:T(512)S(1)} %copy-done.5), kind=kOutput, calls=%fused_computation.12 | convolution fusion | flops 2013462528 | bytes 9963008 | tf_op jit(solution)/shard_map/dot_general | solution.py:109
  204.7 101.5 %all-gather.6.cloned.1.call-done = bf16[512,8192]{1,0:T(8,128)(2,1)} async-done(((bf16[64,8192]{1,0:T(8,128)(2,1)}), bf16[512,8192]{1,0:T(8,128)(2,1)}) %all-gather.6.cloned.1.call-update) | async-done | bytes 8388624 | tf_op jit(solution)/shard_map/all_gather | solution.py:112
  306.2 10.1 %fusion.1 = bf16[512,384]{1,0:T(8,128)(2,1)S(1)} fusion(bf16[512,8192]{1,0:T(8,128)(2,1)} %all-gather.6.cloned.1.call-done, bf16[384,8192]{1,0:T(8,128)(2,1)} %param.14, f32[512,384]{1,0:T(8,128)} %convolution_add_fusion), kind=kOutput, calls=%fused_computation.13 | convolution fusion | flops 3223191552 | bytes 15859712 | tf_op jit(solution)/shard_map/dot_general | solution.py:113
  316.3 0.0 copy-start.6
  316.3 0.7 copy-done.6
  317.0 4.7 convolution_convert_fusion.1
  321.7 0.0 reduce-scatter.4.cloned.1.call-update
  321.8 0.0 reduce-scatter.6.cloned.1.call-start
  321.8 7.4 %convolution_convert_fusion.2 = bf16[5120,384]{1,0:T(8,128)(2,1)} fusion(bf16[512,5120]{1,0:T(8,128)(2,1)} %all-gather.8.cloned.1.call-done, bf16[512,384]{1,0:T(8,128)(2,1)} %copy-done.6), kind=kOutput, calls=%fused_computation.4 | convolution fusion | flops 2015232000 | bytes 9568256 | tf_op jit(solution)/shard_map/dot_general | solution.py:134
  329.3 0.0 reduce-scatter.6.cloned.1.call-update
  329.3 0.3 reduce-scatter.8.cloned.1.call-start
  329.5 9.8 %convolution_convert_fusion = bf16[384,8192]{1,0:T(8,128)(2,1)} fusion(bf16[512,8192]{1,0:T(8,128)(2,1)} %all-gather.6.cloned.1.call-done, f32[512,384]{1,0:T(8,128)} %convolution_add_fusion), kind=kOutput, calls=%fused_computation.2 | convolution fusion | flops 3225354240 | bytes 15466496 | tf_op jit(solution)/shard_map/dot_general | solution.py:117
  339.4 0.0 reduce-scatter.8.cloned.1.call-update
  339.4 71.5 %reduce-scatter.4.cloned.1.call-done = bf16[64,5120]{1,0:T(8,128)(2,1)} async-done(((bf16[512,5120]{1,0:T(8,128)(2,1)}), bf16[64,5120]{1,0:T(8,128)(2,1)}) %reduce-scatter.4.cloned.1.call-update) | async-done | bytes 655376 | tf_op jit(solution)/shard_map/reduce_scatter | solution.py:121
  410.9 2.8 reshape.262
  413.7 2.2 multiply_reduce_fusion.2
  415.9 0.2 sub.102
  416.1 0.2 copy.14
  416.4 0.2 mul.124
  416.7 0.2 copy.15
  416.9 1.1 copy-done
  418.0 0.2 copy-done.2
  418.1 1.3 fusion.6
  419.4 56.2 %reduce-scatter.6.cloned.1.call-done = bf16[320,384]{1,0:T(8,128)(2,1)} async-done(((bf16[5120,384]{1,0:T(8,128)(2,1)}), bf16[320,384]{1,0:T(8,128)(2,1)}) %reduce-scatter.6.cloned.1.call-update) | async-done | bytes 245776 | tf_op jit(solution)/shard_map/reduce_scatter | solution.py:133
  475.6 72.5 %reduce-scatter.8.cloned.1.call-done = bf16[384,512]{1,0:T(8,128)(2,1)} async-done(((bf16[384,8192]{1,0:T(8,128)(2,1)}), bf16[384,512]{1,0:T(8,128)(2,1)}) %reduce-scatter.8.cloned.1.call-update) | async-done | bytes 393232 | tf_op jit(solution)/shard_map/reduce_scatter | solution.py:141
  (20 shorter events, 0.1 us)
Async XLA Ops:
  7.2 106.9 %all-gather.4.cloned.1.call-start = ((), (), s32[]{:S(2)}) async-start(), calls=%async_computation.3 | async-start | bytes 17825792 | tf_op jit(solution)/shard_map/all_gather | solution.py:71
  17.3 1.3 copy-start.1
  18.6 178.6 %all-gather.8.cloned.1.call-start = ((), (), s32[]{:S(2)}) async-start(), calls=%async_computation.5 | async-start | bytes 5898240 | tf_op jit(solution)/shard_map/all_gather | solution.py:86
  20.8 1.3 copy-start.3
  24.5 281.7 %all-gather.6.cloned.1.call-start = ((), (), s32[]{:S(2)}) async-start(), calls=%async_computation.4 | async-start | bytes 9437184 | tf_op jit(solution)/shard_map/all_gather | solution.py:112
  125.1 72.0 %copy-start.5 = (f32[384]{0:T(512)S(1)}, f32[384]{0:T(512)}, u32[]{:S(2)}) copy-start(f32[384]{0:T(512)} %param.13) | copy-start | bytes 4612
  127.6 283.4 %reduce-scatter.4.cloned.1.call-start = ((), (), s32[]{:S(2)}) async-start(), calls=%async_computation.6 | async-start | bytes 5898240 | tf_op jit(solution)/shard_map/reduce_scatter | solution.py:121
  306.2 10.8 %copy-start.4 = (bf16[5120,384]{1,0:T(8,128)(2,1)S(1)}, bf16[5120,384]{1,0:T(8,128)(2,1)}, u32[]{:S(2)}) copy-start(bf16[5120,384]{1,0:T(8,128)(2,1)} %param.12) | copy-start | bytes 11796484
  316.3 0.7 copy-start.6
  321.8 153.9 %reduce-scatter.6.cloned.1.call-start = ((), (), s32[]{:S(2)}) async-start(), calls=%async_computation.7 | async-start | bytes 4177920 | tf_op jit(solution)/shard_map/reduce_scatter | solution.py:133
  329.3 218.8 %reduce-scatter.8.cloned.1.call-start = ((), (), s32[]{:S(2)}) async-start(), calls=%async_computation.8 | async-start | bytes 6684672 | tf_op jit(solution)/shard_map/reduce_scatter | solution.py:141
  416.6 1.3 copy-start
  416.6 1.5 copy-start.2
Sparse Core Ops, SparseCore 0:
  18.7 95.2 all-gather.3
  116.9 80.1 all-gather.7
  199.5 106.6 all-gather.5
  321.9 88.9 reduce-scatter.3
  413.9 61.6 reduce-scatter.5
  478.5 69.5 reduce-scatter.7
where the time goes:
time: 558 us; the launch traced here: 555 us
  waiting for transfers between devices  460 us (82%)
  matrix products  39.6 us (7%)
  local copies, waits for them, and re-layouts  24.4 us (4%)
  other arithmetic  15.8 us (3%)
  between operations  14.3 us (3%)
    all_gather x1, waiting for transfers between devices, local(): piece = lax.all_gather(returned, 'dp', axis=0, tiled=True)  102 us
    all_gather x1, waiting for transfers between devices, return_gradients(): everything = lax.all_gather(packed, 'seq', axis=0, tiled=True)  89 us
    reduce_scatter x1, waiting for transfers between devices, local(): lax.psum_scatter(weight_total.astype(jnp.bfloat16), 'seq', scatter_dimens...  72.5 us
    reduce_scatter x1, waiting for transfers between devices, local(): lax.psum_scatter(lax.dot_general(block, w_in, (((1,), (1,)), ((), ())), p...  71.5 us
    all_gather x1, waiting for transfers between devices, gather_normed(): return lax.all_gather(normalized_rows, 'dp', axis=0, tiled=True)  69.4 us
    reduce_scatter x1, waiting for transfers between devices, local(): lax.psum_scatter(lax.dot_general(block, grad_pre, (((0,), (0,)), ((), ())...  56.2 us
  transfers between devices with their start and end apart: 6, of which 6 were waited for; matrix products, arithmetic and copies ran while one was open for 9% of the time, Pallas kernels for 0%

commit v1 on v0

v1 whole, which is shorter than its diff:
```python
import functools

import jax
import jax.numpy as jnp
from jax import lax
from jax.experimental import pallas as pl
from jax.experimental.pallas import tpu as pltpu
from jax.sharding import PartitionSpec as P

EPS = 1e-06
MESH = pl.DeviceIdType.MESH
BF = jnp.bfloat16
F32 = jnp.float32
D = 8192
MW = 5120
VW = 1280
HID = 384
SLOTS = 64
TOK = 256
HALF = 32
CW = 2048
NT_DIMS = (((1,), (1,)), ((), ()))
TN_DIMS = (((0,), (0,)), ((), ()))


def slot_positions(counts_row, owner_row, starts_row, owners, capacity):
    chosen = owner_row[None, :] == jnp.arange(owners, dtype=jnp.int32)[:, None]
    taken = jnp.where(chosen, counts_row[None, :], 0)
    before = jnp.cumsum(taken, axis=1) - taken
    slots = jnp.arange(capacity, dtype=jnp.int32)
    inside = (
        chosen[:, None, :]
        & (slots[None, :, None] >= before[:, None, :])
        & (slots[None, :, None] < (before + taken)[:, None, :])
    )
    located = jnp.where(
        inside, starts_row[None, None, :] + slots[None, :, None] - before[:, None, :], 0
    )
    return jnp.where(jnp.any(inside, axis=2), jnp.sum(located, axis=2), -1)


def normal_cdf(value):
    return 0.5 * (1.0 + lax.erf(value * 0.7071067811865476))


def normal_pdf(value):
    return jnp.exp(-0.5 * value * value) * 0.3989422804014327


class Place:
    def __init__(self):
        d = lax.axis_index("dp")
        s = lax.axis_index("seq")
        self.x, self.zh = lax.div(d, 2), lax.rem(d, 2)
        self.zl, self.y, self.c = lax.div(s, 8), lax.rem(lax.div(s, 2), 4), lax.rem(s, 2)
        self.XP = self.dev(x=self.xs(1))
        self.XM = self.dev(x=self.xs(3))
        self.YP = self.dev(y=self.ys(1))
        self.YM = self.dev(y=self.ys(3))
        self.ZX = self.dev(zh=1 - self.zh, zl=1 - self.zl)
        self.ZL = self.dev(zl=1 - self.zl)
        self.CO = self.dev(c=1 - self.c)

    def xs(self, k):
        return lax.rem(self.x + k, 4)

    def ys(self, k):
        return lax.rem(self.y + k, 4)

    def dev(self, **kw):
        g = lambda n: kw.get(n, getattr(self, n))
        return (g("x") * 2 + g("zh"), g("zl") * 8 + g("y") * 2 + g("c"))

    def barrier(self):
        bar = pltpu.get_barrier_semaphore()
        everyone = (self.XP, self.XM, self.YP, self.YM, self.ZX, self.ZL, self.CO)
        for to in everyone:
            pl.semaphore_signal(bar, inc=1, device_id=to, device_id_type=MESH)
        pl.semaphore_wait(bar, len(everyone))


class Copies:
    def __init__(self, send, recv):
        self.send, self.recv, self.all = send, recv, []

    def __call__(self, src, dst, to):
        i = len(self.all)
        cp = pltpu.make_async_remote_copy(
            src_ref=src, dst_ref=dst, send_sem=self.send.at[i], recv_sem=self.recv.at[i],
            device_id=to, device_id_type=MESH,
        )
        cp.start()
        self.all.append(cp)
        return cp

    def finish(self):
        for cp in self.all:
            cp.wait_send()


class Gather:
    def __init__(self, pc, copy, buf, lo, w, z_first):
        self.pc, self.copy, self.buf, self.z_first = pc, copy, buf, z_first
        self.cols = pl.ds(lo, w)

    def blk(self, k, z, r=slice(None)):
        return self.buf.at[self.pc.xs(k) * 2 + z, r, self.cols]

    def to(self, ref, where):
        return self.copy(ref, ref, where)

    def s1(self):
        pc = self.pc
        own = self.blk(0, pc.zh)
        if self.z_first:
            self.z = self.to(own, pc.ZX)
        self.p, self.m = self.to(own, pc.XP), self.to(own, pc.XM)
        if not self.z_first:
            self.z = self.to(own, pc.ZX)

    def relay(self, z):
        pc = self.pc
        return [
            self.to(self.blk(3, z, pl.ds(0, HALF)), pc.XP),
            self.to(self.blk(1, z, pl.ds(HALF, HALF)), pc.XM),
        ]

    def s2(self):
        pc = self.pc
        if self.z_first:
            self.z.wait_recv()
            other = self.blk(0, 1 - pc.zh)
            self.zp, self.zm = self.to(other, pc.XP), self.to(other, pc.XM)
        else:
            self.p.wait_recv()
            self.m.wait_recv()
            self.r = self.relay(pc.zh)
            self.f = [self.to(self.blk(3, pc.zh), pc.ZX), self.to(self.blk(1, pc.zh), pc.ZX)]

    def s3(self):
        pc = self.pc
        if self.z_first:
            self.p.wait_recv()
            self.m.wait_recv()
            self.r = self.relay(pc.zh)
        else:
            for cp in self.r:
                cp.wait_recv()
            self.f.append(self.to(self.blk(2, pc.zh), pc.ZX))

    def s4(self):
        if self.z_first:
            self.zp.wait_recv()
            self.zm.wait_recv()
            self.r += self.relay(1 - self.pc.zh)

    def s5(self):
        for cp in self.r if self.z_first else [self.z] + self.f:
            cp.wait_recv()


def gather_kernel(
    pack_ref, route_ref, gain_ref, b_ref, gs_hbm, feat_hbm, win_hbm, wout_hbm,
    rt_hbm, nt_hbm, act_ref, gp_ref,
    gs, feat, win, wout, g, hb, hc, hz, rt, nt, pre, gh,
    send, recv, lsem,
):
    pc = Place()
    copy = Copies(send, recv)
    nc = D // CW
    cut = lambda i: pl.ds(i * CW, CW)
    loads = [
        pltpu.make_async_copy(gs_hbm.at[:, cut(i)], gs.at[:, cut(i)], lsem.at[i]) for i in range(nc)
    ]
    load_feat = pltpu.make_async_copy(feat_hbm, feat, lsem.at[nc])
    load_win = pltpu.make_async_copy(win_hbm, win, lsem.at[nc + 1])
    load_wout = pltpu.make_async_copy(wout_hbm, wout, lsem.at[nc + 2])
    loads[0].start()
    load_feat.start()
    for i in range(1, nc):
        loads[i].start()
    load_win.start()
    load_wout.start()
    stores = []

    def store(src, dst):
        cp = pltpu.make_async_copy(src, dst, lsem.at[nc + 3 + len(stores)])
        cp.start()
        stores.append(cp)

    me = pc.x * 2 + pc.zh
    pc.barrier()
    yp, ym, rp, rm, co, zl = ([None] * nc for _ in range(6))

    def pack(i):
        loads[i].wait()
        g[pc.y, :, cut(i)] = jnp.dot(
            pack_ref[...], gs[:, cut(i)], preferred_element_type=F32
        ).astype(BF)
        own = g.at[pc.y, :, cut(i)]
        yp[i] = copy(own, own, pc.YP)
        ym[i] = copy(own, own, pc.YM)

    def ring(i):
        yp[i].wait_recv()
        up = g.at[pc.ys(3), pl.ds(0, HALF), cut(i)]
        rp[i] = copy(up, up, pc.YP)
        ym[i].wait_recv()
        down = g.at[pc.ys(1), pl.ds(HALF, HALF), cut(i)]
        rm[i] = copy(down, down, pc.YM)

    def route(i):
        rp[i].wait_recv()
        rm[i].wait_recv()
        for j in range(CW // 512):
            cols = pl.ds(i * CW + j * 512, 512)
            hb[:, cols] = jnp.dot(
                route_ref[...], g[:, :, cols].reshape(4 * SLOTS, 512), preferred_element_type=F32
            ).astype(BF)
        co[i] = copy(hb.at[pl.ds(128, 128), cut(i)], hc.at[:, cut(i)], pc.CO)

    def across(i):
        co[i].wait_recv()
        hb[0:128, cut(i)] = hb[0:128, cut(i)] + hc[:, cut(i)]
        zl[i] = copy(hb.at[pl.ds(64, 64), cut(i)], hz.at[:, cut(i)], pc.ZL)

    def arrive(i):
        zl[i].wait_recv()
        rt[me, :, cut(i)] = hb[0:64, cut(i)] + hz[:, cut(i)]
        cs[i].s1()

    ns = [
        Gather(pc, copy, nt, 0, 3072, True),
        Gather(pc, copy, nt, 3072, 2048, False),
    ]
    cs = [Gather(pc, copy, rt, i * CW, CW, i % 2 == 0) for i in range(nc)]

    def normalize():
        load_feat.wait()
        for p in range(4):
            cols = slice(p * VW, (p + 1) * VW)
            v = feat[:, cols].astype(F32)
            d = v - jnp.mean(v, axis=1, keepdims=True)
            inv = lax.rsqrt(jnp.mean(d * d, axis=1, keepdims=True) + EPS)
            nt[me, :, cols] = (d * inv * gain_ref[...]).astype(BF)

    def contract(total, rows, weights, lo, w, dims, by):
        def step(k, _):
            cols = pl.ds(pl.multiple_of(lo + k * by, by), by)
            a = rows[:, :, cols].reshape(8 * SLOTS, by)
            b = weights[:, cols] if dims is NT_DIMS else weights[cols, :]
            if dims is NT_DIMS:
                total[...] += lax.dot_general(a, b, NT_DIMS, preferred_element_type=F32)
            else:
                total[...] += jnp.dot(a, b, preferred_element_type=F32)
            return 0

        lax.fori_loop(0, w // by, step, 0)

    def hidden(i):
        cs[i].s5()
        store(rt.at[:, :, cut(i)], rt_hbm.at[:, :, cut(i)])
        contract(gh, rt, wout, i * CW, CW, NT_DIMS, 1024)

    pack(0)
    pack(1)
    normalize()
    ns[0].s1()
    ns[1].s1()
    ring(0)
    pack(2)
    ring(1)
    route(0)
    pack(3)
    ns[0].s2()
    across(0)
    ring(2)
    route(1)
    arrive(0)
    across(1)
    ns[1].s2()
    ring(3)
    route(2)
    arrive(1)
    across(2)
    ns[0].s3()
    cs[0].s2()
    route(3)
    arrive(2)
    across(3)
    ns[1].s3()
    ns[0].s4()
    arrive(3)
    cs[1].s2()
    cs[0].s3()
    cs[2].s2()
    ns[0].s5()
    ns[1].s5()
    store(nt, nt_hbm)
    cs[0].s4()
    cs[1].s3()
    load_win.wait()
    pre[...] = jnp.broadcast_to(b_ref[...], pre.shape)
    gh[...] = jnp.zeros_like(gh)
    contract(pre, nt, win, 0, MW, None, 512)
    load_wout.wait()
    hidden(0)
    cs[2].s3()
    cs[3].s2()

    def activate(k, _):
        rows = pl.ds(pl.multiple_of(k * 64, 64), 64)
        v = pre[rows, :]
        cdf = normal_cdf(v)
        act_ref[rows, :] = (v * cdf).astype(BF)
        pre[rows, :] = cdf + v * normal_pdf(v)
        return 0

    lax.fori_loop(0, 8, activate, 0)
    hidden(1)
    cs[2].s4()
    cs[3].s3()
    hidden(2)
    hidden(3)

    def finish(k, _):
        rows = pl.ds(pl.multiple_of(k * 64, 64), 64)
        gp_ref[rows, :] = (gh[rows, :] * pre[rows, :]).astype(BF)
        return 0

    lax.fori_loop(0, 8, finish, 0)
    copy.finish()
    for cp in stores:
        cp.wait()


K1_COPIES = 100


def gather_call(pack, route, gain, bias, gs, feat, win, wout):
    vm = pl.BlockSpec(memory_space=pltpu.VMEM)
    hb = pl.BlockSpec(memory_space=pl.ANY)
    return pl.pallas_call(
        gather_kernel,
        out_shape=(
            jax.ShapeDtypeStruct((8, SLOTS, D), BF),
            jax.ShapeDtypeStruct((8, SLOTS, MW), BF),
            jax.ShapeDtypeStruct((8 * SLOTS, HID), BF),
            jax.ShapeDtypeStruct((8 * SLOTS, HID), BF),
        ),
        in_specs=[vm, vm, vm, vm, hb, hb, hb, hb],
        out_specs=(hb, hb, vm, vm),
        scratch_shapes=[
            pltpu.VMEM((TOK, D), BF),
            pltpu.VMEM((SLOTS, MW), BF),
            pltpu.VMEM((MW, HID), BF),
            pltpu.VMEM((HID, D), BF),
            pltpu.VMEM((4, SLOTS, D), BF),
            pltpu.VMEM((4 * SLOTS, D), BF),
            pltpu.VMEM((2 * SLOTS, D), BF),
            pltpu.VMEM((SLOTS, D), BF),
            pltpu.VMEM((8, SLOTS, D), BF),
            pltpu.VMEM((8, SLOTS, MW), BF),
            pltpu.VMEM((8 * SLOTS, HID), F32),
            pltpu.VMEM((8 * SLOTS, HID), F32),
            pltpu.SemaphoreType.DMA((K1_COPIES,)),
            pltpu.SemaphoreType.DMA((K1_COPIES,)),
            pltpu.SemaphoreType.DMA((16,)),
        ],
        compiler_params=pltpu.CompilerParams(
            collective_id=0, has_side_effects=True, vmem_limit_bytes=60 * 2**20
        ),
        cost_estimate=pl.CostEstimate(
            flops=2 * 512 * 384 * 13312, bytes_accessed=30 * 2**20, transcendentals=400000
        ),
        name="gather_rows",
    )(pack, route, gain, bias, gs, feat, win, wout)


class InputScatter:
    def __init__(self, pc, copy, gn, xa, xb, zr, fin, lo, w, x_first):
        self.pc, self.copy, self.gn, self.xa, self.xb, self.zr, self.fin = pc, copy, gn, xa, xb, zr, fin
        self.cols, self.x_first = pl.ds(lo, w), x_first
        self.zs = pl.ds(0, 2) if x_first else pl.ds(pc.zh, 1)

    def s1(self):
        pc, c, gn = self.pc, self.cols, self.gn
        if self.x_first:
            self.first()
        else:
            self.z = self.copy(gn.at[:, 1 - pc.zh, :, c], self.zr.at[:, :, c], pc.ZX)

    def first(self):
        pc, c, gn = self.pc, self.cols, self.gn
        far = pc.xs(2)
        self.a = [
            self.copy(gn.at[far, self.zs, pl.ds(0, HALF), c], self.xa.at[0, self.zs, :, c], pc.XP),
            self.copy(gn.at[far, self.zs, pl.ds(HALF, HALF), c], self.xa.at[1, self.zs, :, c], pc.XM),
        ]

    def second(self):
        pc, c, gn = self.pc, self.cols, self.gn
        self.b = []
        for d, (k, to) in enumerate(((1, pc.XP), (3, pc.XM))):
            self.a[d].wait_recv()
            rows = pl.ds(d * HALF, HALF)
            gn[pc.xs(k), self.zs, rows, c] = gn[pc.xs(k), self.zs, rows, c] + self.xa[d, self.zs, :, c]
            self.b.append(self.copy(gn.at[pc.xs(k), self.zs, :, c], self.xb.at[d, self.zs, :, c], to))

    def s2(self):
        pc, c, gn = self.pc, self.cols, self.gn
        if self.x_first:
            self.second()
        else:
            self.z.wait_recv()
            for k in (2, 1, 3, 0):
                gn[pc.xs(k), pc.zh, :, c] = gn[pc.xs(k), pc.zh, :, c] + self.zr[pc.xs(k), :, c]
                if k == 2:
                    self.first()

    def total(self, z):
        c = self.cols
        return (
            self.gn[self.pc.x, z, :, c].astype(F32)
            + self.xb[0, z, :, c].astype(F32)
            + self.xb[1, z, :, c].astype(F32)
        )

    def s3(self):
        pc, c, gn = self.pc, self.cols, self.gn
        if self.x_first:
            for cp in self.b:
                cp.wait_recv()
            gn[pc.x, 1 - pc.zh, :, c] = self.total(1 - pc.zh).astype(BF)
            self.z = self.copy(gn.at[pc.x, 1 - pc.zh, :, c], self.zr.at[0, :, c], pc.ZX)
        else:
            self.second()

    def s4(self):
        c = self.cols
        if self.x_first:
            self.z.wait_recv()
            self.fin[:, c] = self.total(self.pc.zh) + self.zr[0, :, c].astype(F32)
        else:
            for cp in self.b:
                cp.wait_recv()
            self.fin[:, c] = self.total(self.pc.zh)


class WeightScatter:
    def __init__(self, pc, copy, w, cr, ya, yb, zr, out):
        self.pc, self.copy, self.w, self.cr, self.ya, self.yb, self.zr, self.out = (
            pc, copy, w, cr, ya, yb, zr, out
        )
        self.half = w.shape[3] // 2
        self.co = {}

    def to_core(self, k):
        pc = self.pc
        y = pc.ys(k)
        self.co[k] = self.copy(self.w.at[1 - pc.c, y], self.cr.at[y], pc.CO)

    def add_core(self, k):
        pc = self.pc
        y = pc.ys(k)
        self.co[k].wait_recv()
        for z in range(2):
            self.w[pc.c, y, z] = self.w[pc.c, y, z] + self.cr[y, z]

    def first(self):
        pc, h = self.pc, self.half
        self.add_core(2)
        far = self.w.at[pc.c, pc.ys(2)]
        self.a = [
            self.copy(far.at[:, pl.ds(0, h)], self.ya.at[0], pc.YP),
            self.copy(far.at[:, pl.ds(h, h)], self.ya.at[1], pc.YM),
        ]

    def second(self):
        pc, h = self.pc, self.half
        self.b = []
        for d, (k, to) in enumerate(((1, pc.YP), (3, pc.YM))):
            y = pc.ys(k)
            rows = pl.ds(d * h, h)
            self.add_core(k)
            self.a[d].wait_recv()
            for z in range(2):
                self.w[pc.c, y, z, rows] = self.w[pc.c, y, z, rows] + self.ya[d, z]
            self.b.append(self.copy(self.w.at[pc.c, y], self.yb.at[d], to))

    def total(self, z):
        pc = self.pc
        return (
            self.w[pc.c, pc.y, z].astype(F32)
            + self.yb[0, z].astype(F32)
            + self.yb[1, z].astype(F32)
        )

    def third(self):
        pc = self.pc
        self.add_core(0)
        for cp in self.b:
            cp.wait_recv()
        self.w[pc.c, pc.y, 1 - pc.zl] = self.total(1 - pc.zl).astype(BF)
        self.z = self.copy(self.w.at[pc.c, pc.y, 1 - pc.zl], self.zr, pc.ZL)

    def last(self):
        self.z.wait_recv()
        self.out[...] = (self.total(self.pc.zl) + self.zr[...].astype(F32)).astype(BF)


def scatter_kernel(
    gain_ref, act_ref, gp_ref, rt_hbm, nt_hbm, win_hbm, feat_hbm,
    mig_ref, gw1_ref, gw2_ref,
    rt, nt, win, feat, act_t, gn, xa, xb, zr, fin,
    w2, cr2, ya2, yb2, zr2, w1, cr1, ya1, yb1, zr1,
    send, recv, lsem,
):
    pc = Place()
    copy = Copies(send, recv)
    load_win = pltpu.make_async_copy(win_hbm, win, lsem.at[0])
    load_rt = pltpu.make_async_copy(rt_hbm, rt, lsem.at[1])
    load_nt = pltpu.make_async_copy(nt_hbm, nt, lsem.at[2])
    load_feat = pltpu.make_async_copy(feat_hbm, feat, lsem.at[3])
    for cp in (load_win, load_rt, load_nt, load_feat):
        cp.start()
    pc.barrier()

    gw = 1024
    gs = [
        InputScatter(pc, copy, gn, xa, xb, zr, fin, j * gw, gw, j % 2 == 0) for j in range(MW // gw)
    ]
    load_win.wait()
    for j in (1, 0, 3, 2, 4):
        def tile(k, _, j=j):
            at = pl.multiple_of(j * gw + k * 512, 512)
            gn[:, :, :, pl.ds(at, 512)] = (
                lax.dot_general(gp_ref[...], win[pl.ds(at, 512), :], NT_DIMS, preferred_element_type=F32)
                .astype(BF).reshape(4, 2, SLOTS, 512)
            )
            return 0

        lax.fori_loop(0, gw // 512, tile, 0)
        gs[j].s1()

    s2 = WeightScatter(pc, copy, w2, cr2, ya2, yb2, zr2, gw2_ref)
    s1 = WeightScatter(pc, copy, w1, cr1, ya1, yb1, zr1, gw1_ref)
    act_t[...] = act_ref[...].T
    load_rt.wait()

    def grad2(c, k):
        y = pc.ys(k)

        def tile(z, _):
            cols = pl.ds(pl.multiple_of((z * 8 + y * 2 + c) * 512, 512), 512)
            w2[c, y, z] = jnp.dot(
                act_t[...], rt[:, :, cols].reshape(8 * SLOTS, 512), preferred_element_type=F32
            ).astype(BF)
            return 0

        lax.fori_loop(0, 2, tile, 0)

    def grad1(k):
        y = pc.ys(k)

        def tile(z, _):
            cols = pl.ds(pl.multiple_of((z * 4 + y) * 640, 128), 640)
            part = lax.dot_general(
                nt[:, :, cols].reshape(8 * SLOTS, 640), gp_ref[...], TN_DIMS, preferred_element_type=F32
            ).astype(BF)
            w1[0, y, z] = part[0:320]
            w1[1, y, z] = part[320:640]
            return 0

        lax.fori_loop(0, 2, tile, 0)

    for k in (2, 1, 3, 0):
        grad2(1 - pc.c, k)
        s2.to_core(k)
        if k == 1:
            gs[0].s2()
            gs[1].s2()
    grad2(pc.c, 2)
    s2.first()
    gs[3].s2()
    gs[2].s2()
    grad2(pc.c, 1)
    grad2(pc.c, 3)
    grad2(pc.c, 0)
    gs[1].s3()
    gs[0].s3()
    gs[4].s2()
    load_nt.wait()
    for k in (2, 1):
        grad1(k)
        s1.to_core(k)
    s2.second()
    gs[3].s3()
    gs[2].s3()
    s1.first()
    for k in (3, 0):
        grad1(k)
        s1.to_core(k)
    gs[4].s3()
    s1.second()
    gs[0].s4()
    gs[1].s4()
    s2.third()
    gs[3].s4()
    gs[2].s4()
    gs[4].s4()
    load_feat.wait()
    for p in range(4):
        cols = slice(p * VW, (p + 1) * VW)
        v = feat[:, cols].astype(F32)
        d = v - jnp.mean(v, axis=1, keepdims=True)
        inv = lax.rsqrt(jnp.mean(d * d, axis=1, keepdims=True) + EPS)
        xhat = d * inv
        t = fin[:, cols] * gain_ref[...]
        mig_ref[:, cols] = (
            (t - jnp.mean(t, axis=1, keepdims=True) - xhat * jnp.mean(t * xhat, axis=1, keepdims=True)) * inv
        ).astype(BF)
    s1.third()
    s2.last()
    s1.last()
    copy.finish()


K2_COPIES = 60


def scatter_call(gain, act, gp, rt, nt, win, feat):
    vm = pl.BlockSpec(memory_space=pltpu.VMEM)
    hb = pl.BlockSpec(memory_space=pl.ANY)
    return pl.pallas_call(
        scatter_kernel,
        out_shape=(
            jax.ShapeDtypeStruct((SLOTS, MW), BF),
            jax.ShapeDtypeStruct((320, HID), BF),
            jax.ShapeDtypeStruct((HID, 512), BF),
        ),
        in_specs=[vm, vm, vm, hb, hb, hb, hb],
        out_specs=(vm, vm, vm),
        scratch_shapes=[
            pltpu.VMEM((8, SLOTS, D), BF),
            pltpu.VMEM((8, SLOTS, MW), BF),
            pltpu.VMEM((MW, HID), BF),
            pltpu.VMEM((SLOTS, MW), BF),
            pltpu.VMEM((HID, 8 * SLOTS), BF),
            pltpu.VMEM((4, 2, SLOTS, MW), BF),
            pltpu.VMEM((2, 2, HALF, MW), BF),
            pltpu.VMEM((2, 2, SLOTS, MW), BF),
            pltpu.VMEM((4, SLOTS, MW), BF),
            pltpu.VMEM((SLOTS, MW), F32),
            pltpu.VMEM((2, 4, 2, HID, 512), BF),
            pltpu.VMEM((4, 2, HID, 512), BF),
            pltpu.VMEM((2, 2, HID // 2, 512), BF),
            pltpu.VMEM((2, 2, HID, 512), BF),
            pltpu.VMEM((HID, 512), BF),
            pltpu.VMEM((2, 4, 2, 320, HID), BF),
            pltpu.VMEM((4, 2, 320, HID), BF),
            pltpu.VMEM((2, 2, 160, HID), BF),
            pltpu.VMEM((2, 2, 320, HID), BF),
            pltpu.VMEM((320, HID), BF),
            pltpu.SemaphoreType.DMA((K2_COPIES,)),
            pltpu.SemaphoreType.DMA((K2_COPIES,)),
            pltpu.SemaphoreType.DMA((4,)),
        ],
        compiler_params=pltpu.CompilerParams(
            collective_id=1, has_side_effects=True, vmem_limit_bytes=62 * 2**20
        ),
        cost_estimate=pl.CostEstimate(
            flops=2 * 512 * 384 * 18432, bytes_accessed=30 * 2**20, transcendentals=400
        ),
        name="scatter_sums",
    )(gain, act, gp, rt, nt, win, feat)


def local(
    grad_seq, features, merger_norm_gain, w_in, b_in, w_out, image_counts, sample_owner, image_starts
):
    seq_index = lax.axis_index("seq")
    zl, y, c = seq_index // 8, (seq_index // 2) % 4, seq_index % 2
    counts, owner, starts = image_counts[0], sample_owner[0], image_starts[0]
    wanted = slot_positions(counts, owner, starts, 16, SLOTS)
    packing = slot_positions(counts, starts // TOK, starts, 16, SLOTS)
    mine = lax.dynamic_index_in_dim(packing, seq_index, 0, False)
    places = seq_index * TOK + jnp.arange(TOK, dtype=jnp.int32)
    pack = (mine[:, None] == places[None, :]).astype(BF)
    want = lax.dynamic_index_in_dim(wanted.reshape(2, 4, 2, SLOTS), y, 1, False)
    pair = lambda a, i: jnp.concatenate(
        [lax.dynamic_index_in_dim(a, i, 0), lax.dynamic_index_in_dim(a, 1 - i, 0)], axis=0
    )
    want = pair(pair(want, zl).transpose(1, 0, 2), c).reshape(-1)
    held = lax.dynamic_index_in_dim(packing.reshape(2, 4, 2, SLOTS), zl, 0, False)
    held = lax.dynamic_index_in_dim(held, c, 1, False).reshape(-1)
    route = ((want[:, None] == held[None, :]) & (want >= 0)[:, None]).astype(BF)
    gain = merger_norm_gain[None, :]
    feat = features[0]
    rt, nt, act, gp = gather_call(pack, route, gain, b_in[None, :], grad_seq[0], feat, w_in, w_out)
    mig, gw1, gw2 = scatter_call(gain, act, gp, rt, nt, w_in, feat)
    return (mig[None], gw1, gw2)


def solution(mesh):
    in_specs = (
        P("dp", "seq", None),
        P("dp", "seq", None),
        P(),
        P(None, "dp"),
        P("dp"),
        P("dp", None),
        P("dp", None),
        P("dp", None),
        P("dp", None),
    )
    out_specs = (P("dp", "seq", None), P("seq", "dp"), P("dp", "seq"))
    return jax.shard_map(local, mesh=mesh, in_specs=in_specs, out_specs=out_specs, check_vma=False)
```

time: 558 us -> 205 us (0.37)
  waiting for transfers between devices: 460 us -> 0 us
  Pallas kernels: 0 us -> 187 us
  matrix products: 39.6 us -> 0 us
  local copies, waits for them, and re-layouts: 24.4 us -> 8.12 us
  between operations: 14.3 us -> 0.78 us
  other arithmetic: 15.8 us -> 6.57 us
    all_gather x3 -> x0, waiting for transfers between devices: 260 us -> none  [the longest x1 102 us: local(): piece = lax.all_gather(returned, 'dp', axis=0, tiled=True)]
    reduce_scatter x3 -> x0, waiting for transfers between devices: 200 us -> none  [the longest x1 72.5 us: local(): lax.psum_scatter(weight_total.astype(jnp.bfloat16), 'seq', scatter_dimens...]
    pallas_call x0 -> x2, Pallas kernels: none -> 187 us  [the longest x1 114 us: gather_call(): pl.pallas_call(gather_kernel, out_shape=(jax.ShapeDtypeStruct((8, SLOTS,...]
    dot_general x5 -> x0, matrix products: 39.6 us -> none  [the longest x1 10.1 us: local(): lax.dot_general(piece, w_out, (((1,), (1,)), ((), ())), preferred_element...]
    gather x2 -> x0, local copies, waits for them, and re-layouts: 16 us -> none  [the longest x1 11.1 us: return_gradients(): jnp.take(everything, index, axis=0)]
  transfers between devices with their start and end apart: 6 -> 0, of which waited for: 6 -> 0; matrix products, arithmetic and copies ran while one was open for 9% -> 0% of each run, Pallas kernels for 0% -> 0%
where the time goes in v1:
time: 205 us; the launch traced here: 202 us
  Pallas kernels  187 us (91%)
  local copies, waits for them, and re-layouts  8.12 us (4%)
  other arithmetic  6.57 us (3%)
    pallas_call x1, Pallas kernels, gather_call(): pl.pallas_call(gather_kernel, out_shape=(jax.ShapeDtypeStruct((8, SLOTS,...  114 us
    pallas_call x1, Pallas kernels, scatter_call(): pl.pallas_call(scatter_kernel, out_shape=(jax.ShapeDtypeStruct((SLOTS, MW...  72.6 us
    unnamed x3, local copies, waits for them, and re-layouts  5.39 us

profile of v1, /device:TPU:1, one launch (start us, length us, event | category | flops | bytes accessed | tf_op | source)
XLA Modules:
  0.0 202.2 jit_solution(6264315328840845825)
XLA Ops:
  0.7 0.7 fusion.13
  1.4 1.2 broadcast_in_dim.63.b_ref
  2.6 0.7 iota_compare_fusion.4
  3.3 1.3 broadcast_in_dim.34.gain_ref
  4.6 0.7 broadcast_select_fusion.2
  5.2 0.2 reduce_window_sum.18
  5.5 0.2 reduce_window_sum.17
  5.7 0.7 fusion.7
  6.4 0.6 fusion.4
  7.0 0.7 iota_add_fusion
  7.7 0.6 select_reduce_fusion
  8.4 0.1 eq.91
  8.5 0.1 eq.93
  8.6 0.7 compare_convert_fusion.pack_ref
  9.3 0.8 and_convert_fusion.route_ref
  10.1 114.1 %gather_rows.1 = (bf16[8,64,8192]{2,1,0:T(8,128)(2,1)}, bf16[8,64,5120]{2,1,0:T(8,128)(2,1)}, bf16[512,384]{1,0:T(8,128)(2,1)}, bf16[512,384]{1,0:T(8,128)(2,1)}) custom-call(bf16[64,256]{1,0:T(8,128)(2,1)} %compare_convert_fusion.pack_ref, bf16[256,256]{1,0:T(8,128)(2,1)} %and_convert_fusion.route_ref, f32[1,1280]{1,0:T(1,128)} %broadcast_in_dim.34.gain_ref, ...), custom_call_target="tpu_custom_call" | custom-call | flops 5234491392 | bytes 31457280 | tf_op jit(solution)/shard_map/gather_rows/pallas_call | solution.py:343
  124.2 72.6 %scatter_sums.1 = (bf16[64,5120]{1,0:T(8,128)(2,1)}, bf16[320,384]{1,0:T(8,128)(2,1)}, bf16[384,512]{1,0:T(8,128)(2,1)}) custom-call(f32[1,1280]{1,0:T(1,128)} %broadcast_in_dim.34.gain_ref, bf16[512,384]{1,0:T(8,128)(2,1)} %get-tuple-element.10.act_ref, bf16[512,384]{1,0:T(8,128)(2,1)} %get-tuple-element.11.gp_ref, ...), custom_call_target="tpu_custom_call" | custom-call | flops 7247757312 | bytes 31457280 | tf_op jit(solution)/shard_map/scatter_sums/pallas_call | solution.py:635
  196.8 2.0 copy.15
  198.8 1.7 copy.16
  200.4 1.8 copy.17
  (10 shorter events, 0.1 us)

commit v2 on v0

v2 whole, which is shorter than its diff:
```python
import jax
import jax.numpy as jnp
from jax import lax
from jax.experimental import pallas as pl
from jax.experimental.pallas import tpu as pltpu
from jax.sharding import PartitionSpec as P

EPS = 1e-06
MESH = pl.DeviceIdType.MESH
BF = jnp.bfloat16
F32 = jnp.float32
I32 = jnp.int32
D = 8192
MW = 5120
VW = 1280
HID = 384
HH = HID // 2
SLOTS = 64
TOK = 256
ROWS = 512
HALF = 32
BW = 512
CW = 1024
GW = 640
NT_DIMS = (((1,), (1,)), ((), ()))
TN_DIMS = (((0,), (0,)), ((), ()))
N_KINDS = "ABAA"
C_KINDS = "BABABABA"
G_KINDS = "ABAABABA"
ORDER = (
    ("norm", 0), ("norm", 1), ("norm", 2), ("norm", 3), ("pack", 0), ("pack", 1), ("pack", 2), ("N3", 0),
    ("N2", 0), ("ring", 0), ("pack", 3), ("N2", 1), ("ring", 1), ("pack", 4), ("N3", 2), ("N2", 2),
    ("ring", 2), ("pack", 5), ("route", 0), ("N3", 3), ("N2", 3), ("across", 0), ("ring", 3), ("pack", 6),
    ("route", 1), ("across", 1), ("arrive", 0), ("N4", 0), ("ring", 4), ("pack", 7), ("N3", 1), ("route", 2),
    ("across", 2), ("arrive", 1), ("ring", 5), ("route", 3), ("N4", 2), ("across", 3), ("arrive", 2),
    ("N5", 1), ("pre", 1), ("ring", 6), ("route", 4), ("C2", 1), ("across", 4), ("arrive", 3), ("N4", 3),
    ("ring", 7), ("route", 5), ("C2", 0), ("route", 6), ("arrive", 4), ("C2", 3), ("N5", 0), ("pre", 0),
    ("route", 7), ("across", 5), ("C3", 1), ("across", 6), ("across", 7), ("N5", 2), ("pre", 2),
    ("arrive", 5), ("C2", 2), ("arrive", 6), ("C4", 1), ("C2", 5), ("arrive", 7), ("C3", 3), ("N5", 3),
    ("pre", 3), ("act", 0), ("C3", 0), ("C2", 4), ("C4", 3), ("C2", 7), ("C5", 0), ("hid", 0), ("C3", 5),
    ("C3", 2), ("C2", 6), ("C5", 1), ("w2", 0), ("hid", 1), ("C4", 5), ("C5", 2), ("hid", 2), ("w2a", 0),
    ("C3", 7), ("C3", 4), ("w2b", 0), ("C5", 3), ("w2", 1), ("hid", 3), ("C4", 7), ("C5", 4), ("hid", 4),
    ("w2a", 1), ("w2c", 0), ("C3", 6), ("C5", 5), ("w2", 2), ("w2b", 1), ("hid", 5), ("w2a", 2), ("C5", 7),
    ("hid", 7), ("C5", 6), ("hid", 6), ("gp", 0), ("gn", 0), ("w2c", 1), ("w2z", 0), ("w2", 3), ("w2b", 2),
    ("g2", 0), ("gn", 1), ("gn", 2), ("w2a", 3), ("gn", 3), ("g1", 2), ("w2s", 0), ("gn", 4), ("gn", 5),
    ("f1", 0), ("w2c", 2), ("g1", 1), ("g2", 2), ("g2", 3), ("w2b", 3), ("g2", 1), ("g1", 3), ("g2", 5),
    ("gn", 6), ("g3", 0), ("gn", 7), ("f2", 0), ("g1", 0), ("g3", 2), ("g2", 4), ("w2c", 3), ("w2z", 1),
    ("g3", 3), ("g3", 1), ("g3", 5), ("w2s", 1), ("g2", 7), ("g2", 6), ("w2o", 0), ("g3", 4), ("g4", 0),
    ("w2f", 0), ("g4", 1), ("mig", 0), ("g4", 2), ("f3", 0), ("g4", 3), ("mig", 1), ("g3", 7), ("g4", 5),
    ("g3", 6), ("g4", 4), ("mig", 2), ("g4", 7), ("g4", 6), ("mig", 3), ("f4", 0),
)
MAX_COPIES = 256


def normal_cdf(value):
    return 0.5 * (1.0 + lax.erf(value * 0.7071067811865476))


def normal_pdf(value):
    return jnp.exp(-0.5 * value * value) * 0.3989422804014327


def dot(a, b):
    return jnp.dot(a, b, preferred_element_type=F32)


class Place:
    def __init__(self):
        d = lax.axis_index("dp")
        s = lax.axis_index("seq")
        self.seq = s
        self.x, self.zh = lax.div(d, 2), lax.rem(d, 2)
        self.zl, self.y, self.c = lax.div(s, 8), lax.rem(lax.div(s, 2), 4), lax.rem(s, 2)
        self.XP = self.dev(x=self.xs(1))
        self.XM = self.dev(x=self.xs(3))
        self.YP = self.dev(y=self.ys(1))
        self.YM = self.dev(y=self.ys(3))
        self.ZX = self.dev(zh=1 - self.zh, zl=1 - self.zl)
        self.ZL = self.dev(zl=1 - self.zl)
        self.CO = self.dev(c=1 - self.c)

    def xs(self, k):
        return lax.rem(self.x + k, 4)

    def ys(self, k):
        return lax.rem(self.y + k, 4)

    def dev(self, **kw):
        g = lambda n: kw.get(n, getattr(self, n))
        return (g("x") * 2 + g("zh"), g("zl") * 8 + g("y") * 2 + g("c"))

    def barrier(self):
        bar = pltpu.get_barrier_semaphore()
        everyone = (self.XP, self.XM, self.YP, self.YM, self.ZX, self.ZL, self.CO)
        for to in everyone:
            pl.semaphore_signal(bar, inc=1, device_id=to, device_id_type=MESH)
        pl.semaphore_wait(bar, len(everyone))


class Copies:
    def __init__(self, send, recv):
        self.send, self.recv, self.all, self.sent = send, recv, [], set()

    def __call__(self, src, dst, to):
        i = len(self.all)
        cp = pltpu.make_async_remote_copy(
            src_ref=src, dst_ref=dst, send_sem=self.send.at[i], recv_sem=self.recv.at[i],
            device_id=to, device_id_type=MESH,
        )
        cp.start()
        self.all.append(cp)
        return cp

    def leave(self, copies):
        for cp in copies:
            if id(cp) not in self.sent:
                self.sent.add(id(cp))
                cp.wait_send()

    def finish(self):
        self.leave(self.all)


class Gather:
    def __init__(self, pc, copy, buf, lo, w, z_first):
        self.pc, self.copy, self.buf, self.z_first = pc, copy, buf, z_first
        self.cols = pl.ds(lo, w)

    def blk(self, k, z, r=slice(None)):
        return self.buf.at[self.pc.xs(k) * 2 + z, r, self.cols]

    def to(self, ref, where):
        return self.copy(ref, ref, where)

    def s1(self):
        pc = self.pc
        own = self.blk(0, pc.zh)
        if self.z_first:
            self.z = self.to(own, pc.ZX)
        self.p, self.m = self.to(own, pc.XP), self.to(own, pc.XM)
        if not self.z_first:
            self.z = self.to(own, pc.ZX)

    def relay(self, z):
        pc = self.pc
        return [
            self.to(self.blk(3, z, pl.ds(0, HALF)), pc.XP),
            self.to(self.blk(1, z, pl.ds(HALF, HALF)), pc.XM),
        ]

    def s2(self):
        pc = self.pc
        if self.z_first:
            self.z.wait_recv()
            other = self.blk(0, 1 - pc.zh)
            self.zp, self.zm = self.to(other, pc.XP), self.to(other, pc.XM)
        else:
            self.p.wait_recv()
            self.m.wait_recv()
            self.r = self.relay(pc.zh)
            self.f = [self.to(self.blk(3, pc.zh), pc.ZX), self.to(self.blk(1, pc.zh), pc.ZX)]

    def s3(self):
        pc = self.pc
        if self.z_first:
            self.p.wait_recv()
            self.m.wait_recv()
            self.r = self.relay(pc.zh)
        else:
            for cp in self.r:
                cp.wait_recv()
            self.f.append(self.to(self.blk(2, pc.zh), pc.ZX))

    def s4(self):
        self.zp.wait_recv()
        self.zm.wait_recv()
        self.r += self.relay(1 - self.pc.zh)

    def s5(self):
        for cp in self.r if self.z_first else [self.z] + self.f:
            cp.wait_recv()


class InputScatter:
    def __init__(self, pc, copy, gn, xa, xb, zr, fin, lo, at, w, x_first):
        self.pc, self.copy, self.gn, self.xa, self.xb, self.zr, self.fin = pc, copy, gn, xa, xb, zr, fin
        self.cols, self.at, self.x_first = pl.ds(lo, w), pl.ds(at, w), x_first
        self.zs = pl.ds(0, 2) if x_first else pl.ds(pc.zh, 1)

    def s1(self):
        pc, c = self.pc, self.cols
        if self.x_first:
            self.first()
        else:
            self.z = self.copy(self.gn.at[:, 1 - pc.zh, :, c], self.zr.at[:, :, self.at], pc.ZX)

    def first(self):
        pc, c, gn, at = self.pc, self.cols, self.gn, self.at
        far = pc.xs(2)
        self.a = [
            self.copy(gn.at[far, self.zs, pl.ds(0, HALF), c], self.xa.at[0, :, :, at], pc.XP),
            self.copy(gn.at[far, self.zs, pl.ds(HALF, HALF), c], self.xa.at[1, :, :, at], pc.XM),
        ]

    def second(self):
        pc, c, gn, at = self.pc, self.cols, self.gn, self.at
        self.b = []
        for d, (k, to) in enumerate(((1, pc.XP), (3, pc.XM))):
            self.a[d].wait_recv()
            rows = pl.ds(d * HALF, HALF)
            gn[pc.xs(k), self.zs, rows, c] = gn[pc.xs(k), self.zs, rows, c] + self.xa[d, :, :, at]
            self.b.append(self.copy(gn.at[pc.xs(k), self.zs, :, c], self.xb.at[d, :, :, at], to))

    def s2(self):
        pc, c, gn = self.pc, self.cols, self.gn
        if self.x_first:
            self.second()
        else:
            self.z.wait_recv()
            for k in (2, 1, 3, 0):
                gn[pc.xs(k), pc.zh, :, c] = gn[pc.xs(k), pc.zh, :, c] + self.zr[pc.xs(k), :, self.at]
                if k == 2:
                    self.first()

    def total(self, z):
        i = z if self.x_first else 0
        return (
            self.gn[self.pc.x, z, :, self.cols].astype(F32)
            + self.xb[0, i, :, self.at].astype(F32)
            + self.xb[1, i, :, self.at].astype(F32)
        )

    def s3(self):
        pc, c, gn = self.pc, self.cols, self.gn
        if self.x_first:
            for cp in self.b:
                cp.wait_recv()
            gn[pc.x, 1 - pc.zh, :, c] = self.total(1 - pc.zh).astype(BF)
            self.z = self.copy(gn.at[pc.x, 1 - pc.zh, :, c], self.zr.at[:, self.at], pc.ZX)
        else:
            self.second()

    def s4(self):
        if self.x_first:
            self.z.wait_recv()
            self.fin[:, self.cols] = self.total(self.pc.zh) + self.zr[:, self.at].astype(F32)
        else:
            for cp in self.b:
                cp.wait_recv()
            self.fin[:, self.cols] = self.total(self.pc.zh)


def routing_tables(pc, cnt, own, st):
    iota = lambda shape, axis: lax.broadcasted_iota(I32, shape, axis)
    one = lambda m: jnp.where(m, 1.0, 0.0).astype(BF)
    i0, i1 = iota((64, 64), 0), iota((64, 64), 1)
    col = lambda r: jnp.sum(jnp.where(i0 == i1, r, 0), axis=1, keepdims=True)
    sh = lax.div(st, TOK)
    cnt_c, own_c, st_c, sh_c = col(cnt), col(own), col(st), col(sh)
    before_o = jnp.sum(jnp.where((own_c == own) & (i0 < i1), cnt_c, 0), axis=0, keepdims=True)
    before_h = jnp.sum(jnp.where((sh_c == sh) & (i1 < i0), cnt, 0), axis=1, keepdims=True)
    off = iota((64, TOK), 1) + pc.seq * TOK - st_c
    inside = (sh_c == pc.seq) & (off >= 0) & (off < cnt_c)
    rank = jnp.sum(jnp.where(inside, before_h + off + 1, 0), axis=0, keepdims=True) - 1
    pack = one(iota((64, TOK), 0) == rank)
    r = iota((256, 64), 0)
    q, k = lax.div(r, 64), lax.rem(r, 64)
    core = pc.c + lax.div(q, 2) * (1 - 2 * pc.c)
    zl = pc.zl + lax.rem(q, 2) * (1 - 2 * pc.zl)
    off = k - before_o
    inside = (own == zl * 8 + pc.y * 2 + core) & (off >= 0) & (off < cnt)
    want = jnp.sum(jnp.where(inside, st + off + 1, 0), axis=1, keepdims=True)
    r = iota((64, 256), 1)
    off = lax.rem(r, 64) - before_h
    inside = (sh_c == pc.zl * 8 + lax.div(r, 64) * 2 + pc.c) & (off >= 0) & (off < cnt_c)
    held = jnp.sum(jnp.where(inside, st_c + off + 1, 0), axis=0, keepdims=True)
    return pack, one((want == held) & (want > 0))


def merger_kernel(
    cnt_ref, own_ref, st_ref, gain_ref, b_ref, gs_hbm, feat_hbm, win_hbm, wout_hbm,
    mig_ref, gw1_ref, gw2_ref,
    pack_m, route_m, big, feat, win, wout, g, hc, hz, rt, nt, pre, gh, act_t, gp,
    w2, cr2, ya2, yb2, ss, zr2, o2, xaa, xba, zra, xab, xbb, zrb, fin, cr1, ya1, yb1, zr1,
    send, recv, lsem,
):
    pc = Place()
    copy = Copies(send, recv)
    me = pc.x * 2 + pc.zh
    nc = D // CW
    cut = lambda i: pl.ds(i * CW, CW)
    loads = []

    def load(src, dst):
        cp = pltpu.make_async_copy(src, dst, lsem.at[len(loads)])
        cp.start()
        loads.append(cp)
        return cp

    def piece(p):
        return pl.ds(((p // 4) % 2 * 8 + p % 4 * 2 + p // 8) * BW, BW)

    lf = load(feat_hbm, feat)
    lg = [load(gs_hbm.at[:, :, :, piece(p)], big.at[0:2, :, :, pl.ds(p * BW, BW)]) for p in range(16)]
    lw = load(win_hbm, win)
    lo = [load(wout_hbm.at[:, piece(p)], wout.at[p]) for p in range(16)]
    pack_m[...], route_m[...] = routing_tables(pc, cnt_ref[...], own_ref[...], st_ref[...])
    gain = gain_ref[...].reshape(1, VW)
    pc.barrier()

    yp, ym, rp, rm, co, zl = ({} for _ in range(6))

    def do_pack(i):
        lg[2 * i].wait()
        lg[2 * i + 1].wait()
        g[pc.y, :, cut(i)] = dot(pack_m[...], big[0:2, :, :, cut(i)].reshape(TOK, CW)).astype(BF)
        own = g.at[pc.y, :, cut(i)]
        yp[i] = copy(own, own, pc.YP)
        ym[i] = copy(own, own, pc.YM)

    def do_ring(i):
        yp[i].wait_recv()
        up = g.at[pc.ys(3), pl.ds(0, HALF), cut(i)]
        rp[i] = copy(up, up, pc.YP)
        ym[i].wait_recv()
        down = g.at[pc.ys(1), pl.ds(HALF, HALF), cut(i)]
        rm[i] = copy(down, down, pc.YM)

    def do_route(i):
        rp[i].wait_recv()
        rm[i].wait_recv()
        for j in range(CW // 512):
            cols = pl.ds(i * CW + j * 512, 512)
            big[2:4, :, :, cols] = (
                dot(route_m[...], g[:, :, cols].reshape(4 * SLOTS, 512)).astype(BF).reshape(2, 2, SLOTS, 512)
            )
        co[i] = copy(big.at[3, :, :, cut(i)], hc.at[:, :, cut(i)], pc.CO)

    def do_across(i):
        co[i].wait_recv()
        big[2, :, :, cut(i)] = big[2, :, :, cut(i)] + hc[:, :, cut(i)]
        zl[i] = copy(big.at[2, 1, :, cut(i)], hz.at[:, cut(i)], pc.ZL)

    cs = [Gather(pc, copy, rt, i * CW, CW, C_KINDS[i] == "A") for i in range(nc)]
    ns = [Gather(pc, copy, nt, n * VW, VW, N_KINDS[n] == "A") for n in range(4)]

    def do_arrive(i):
        zl[i].wait_recv()
        rt[me, :, cut(i)] = big[2, 0, :, cut(i)] + hz[:, cut(i)]
        cs[i].s1()

    def standardized(n):
        v = feat[:, n * VW:(n + 1) * VW].astype(F32)
        d = v - jnp.mean(v, axis=1, keepdims=True)
        inv = lax.rsqrt(jnp.mean(d * d, axis=1, keepdims=True) + EPS)
        return d * inv, inv

    def do_norm(n):
        if n == 0:
            lf.wait()
        nt[me, :, n * VW:(n + 1) * VW] = (standardized(n)[0] * gain).astype(BF)
        ns[n].s1()

    started = []

    def do_pre(n):
        if not started:
            lw.wait()
            pre[...] = jnp.broadcast_to(b_ref[...].reshape(1, HID), pre.shape)
            started.append(n)

        def tile(k, _):
            cols = pl.ds(pl.multiple_of(n * VW + k * 256, 256), 256)
            pre[...] += dot(nt[:, :, cols].reshape(ROWS, 256), win[cols, :])
            return 0

        lax.fori_loop(0, VW // 256, tile, 0)

    def do_act(_):
        def tile(k, _):
            rows = pl.ds(pl.multiple_of(k * 128, 128), 128)
            v = pre[rows, :]
            cdf = normal_cdf(v)
            act_t[:, rows] = (v * cdf).T.astype(BF)
            pre[rows, :] = cdf + v * normal_pdf(v)
            return 0

        lax.fori_loop(0, ROWS // 128, tile, 0)

    opened = []

    def do_hid(i):
        lo[2 * i].wait()
        lo[2 * i + 1].wait()
        for p in (2 * i, 2 * i + 1):
            part = lax.dot_general(
                rt[:, :, p * BW:(p + 1) * BW].reshape(ROWS, BW), wout[p], NT_DIMS, preferred_element_type=F32
            )
            if opened:
                gh[...] += part
            else:
                gh[...] = part
                opened.append(p)

    mine = pl.ds(pl.multiple_of(pc.c * HH, HH), HH)
    theirs = pl.ds(pl.multiple_of((1 - pc.c) * HH, HH), HH)
    wc, wa, wb, wz, wo = ({} for _ in range(5))

    def do_w2(k):
        b = k % 2
        if k >= 2:
            copy.leave([wc[k - 2]] + wa[k - 2] + wb[k - 2])

        def tile(y, _):
            cols = pl.ds(pl.multiple_of(k * 4 * BW + y * BW, BW), BW)
            w2[b, y] = dot(act_t[...], rt[:, :, cols].reshape(ROWS, BW)).astype(BF)
            return 0

        lax.fori_loop(0, 4, tile, 0)
        wc[k] = copy(w2.at[b, :, theirs], cr2.at[k], pc.CO)

    def do_w2a(k):
        b, y = k % 2, pc.ys(2)
        wc[k].wait_recv()
        w2[b, y, mine] = w2[b, y, mine] + cr2[k, y]
        wa[k] = []
        for d, to in enumerate((pc.YP, pc.YM)):
            rows = pl.ds(pl.multiple_of(pc.c * HH + d * HH // 2, HH // 2), HH // 2)
            wa[k].append(copy(w2.at[b, y, rows], ya2.at[k, d], to))

    def do_w2b(k):
        b = k % 2
        wb[k] = []
        for d, (r, to) in enumerate(((1, pc.YP), (3, pc.YM))):
            y = pc.ys(r)
            w2[b, y, mine] = w2[b, y, mine] + cr2[k, y]
            wa[k][d].wait_recv()
            rows = pl.ds(pl.multiple_of(pc.c * HH + d * HH // 2, HH // 2), HH // 2)
            w2[b, y, rows] = w2[b, y, rows] + ya2[k, d]
            wb[k].append(copy(w2.at[b, y, mine], yb2.at[k, d], to))

    def do_w2c(k):
        for cp in wb[k]:
            cp.wait_recv()
        ss[k] = (
            w2[k % 2, pc.y, mine].astype(F32) + cr2[k, pc.y].astype(F32)
            + yb2[k, 0].astype(F32) + yb2[k, 1].astype(F32)
        ).astype(BF)

    def do_w2z(q):
        wz[q] = copy(ss.at[1 - pc.zl + 2 * q], zr2.at[q], pc.ZL)

    def do_w2s(q):
        wz[q].wait_recv()
        ss[pc.zl + 2 * q] = ss[pc.zl + 2 * q] + zr2[q]

    def do_w2o(_):
        wo[0] = copy(ss.at[pc.zl + 2 * (1 - pc.c)], o2, pc.CO)

    def do_w2f(_):
        wo[0].wait_recv()
        gw2_ref[mine, :] = ss[pc.zl + 2 * pc.c]
        gw2_ref[theirs, :] = o2[...]

    def do_gp(_):
        def tile(k, _):
            rows = pl.ds(pl.multiple_of(k * 64, 64), 64)
            gp[rows, :] = (gh[rows, :] * pre[rows, :]).astype(BF)
            return 0

        lax.fori_loop(0, 8, tile, 0)
        copy.leave(list(co.values()) + list(zl.values()))

    gs, used = [], {"A": 0, "B": 0}
    for j, kind in enumerate(G_KINDS):
        xa, xb, zr = (xaa, xba, zra) if kind == "A" else (xab, xbb, zrb)
        gs.append(InputScatter(pc, copy, big, xa, xb, zr, fin, j * GW, used[kind], GW, kind == "A"))
        used[kind] += GW

    def do_gn(j):
        part = lax.dot_general(gp[...], win[j * GW:(j + 1) * GW, :], NT_DIMS, preferred_element_type=F32)
        big[:, :, :, j * GW:(j + 1) * GW] = part.astype(BF).reshape(4, 2, SLOTS, GW)
        gs[j].s1()

    def do_mig(n):
        xhat, inv = standardized(n)
        t = fin[:, n * VW:(n + 1) * VW] * gain
        mig_ref[:, n * VW:(n + 1) * VW] = (
            (t - jnp.mean(t, axis=1, keepdims=True) - xhat * jnp.mean(t * xhat, axis=1, keepdims=True)) * inv
        ).astype(BF)

    vc, va, vb, vz = {}, [], [], []

    def w1(c, y, z, lo=0, n=320):
        return wout.at[c * 8 + y * 2 + z, pl.ds(lo, n), pl.ds(0, HID)]

    def do_g1(k):
        y = pc.ys(k)

        def tile(z, _):
            cols = pl.ds(pl.multiple_of((z * 4 + y) * 640, 128), 640)
            part = lax.dot_general(
                nt[:, :, cols].reshape(ROWS, 640), gp[...], TN_DIMS, preferred_element_type=F32
            ).astype(BF)
            w1(0, y, z)[...] = part[0:320]
            w1(1, y, z)[...] = part[320:640]
            return 0

        lax.fori_loop(0, 2, tile, 0)
        at = pl.ds((1 - pc.c) * 8 + y * 2, 2)
        vc[k] = copy(wout.at[at, pl.ds(0, 320), pl.ds(0, HID)], cr1.at[y], pc.CO)

    def w1_pair(y, lo, n):
        return wout.at[pl.ds(pc.c * 8 + y * 2, 2), pl.ds(lo, n), pl.ds(0, HID)]

    def w1_core(k):
        y = pc.ys(k)
        vc[k].wait_recv()
        for z in range(2):
            w1(pc.c, y, z)[...] = w1(pc.c, y, z)[...] + cr1[y, z]

    def do_f1(_):
        w1_core(2)
        for d, to in enumerate((pc.YP, pc.YM)):
            va.append(copy(w1_pair(pc.ys(2), d * 160, 160), ya1.at[d], to))

    def do_f2(_):
        for d, (r, to) in enumerate(((1, pc.YP), (3, pc.YM))):
            y = pc.ys(r)
            w1_core(r)
            va[d].wait_recv()
            for z in range(2):
                part = w1(pc.c, y, z, d * 160, 160)
                part[...] = part[...] + ya1[d, z]
            vb.append(copy(w1_pair(y, 0, 320), yb1.at[d], to))

    def w1_total(z):
        return w1(pc.c, pc.y, z)[...].astype(F32) + yb1[0, z].astype(F32) + yb1[1, z].astype(F32)

    def do_f3(_):
        w1_core(0)
        for cp in vb:
            cp.wait_recv()
        there = w1(pc.c, pc.y, 1 - pc.zl)
        there[...] = w1_total(1 - pc.zl).astype(BF)
        vz.append(copy(there, zr1, pc.ZL))

    def do_f4(_):
        vz[0].wait_recv()
        gw1_ref[...] = (w1_total(pc.zl) + zr1[...].astype(F32)).astype(BF)

    stages = {
        "pack": do_pack, "ring": do_ring, "route": do_route, "across": do_across, "arrive": do_arrive,
        "norm": do_norm, "pre": do_pre, "act": do_act, "hid": do_hid, "gp": do_gp, "gn": do_gn, "mig": do_mig,
        "w2": do_w2, "w2a": do_w2a, "w2b": do_w2b, "w2c": do_w2c, "w2z": do_w2z, "w2s": do_w2s,
        "w2o": do_w2o, "w2f": do_w2f, "g1": do_g1, "f1": do_f1, "f2": do_f2, "f3": do_f3, "f4": do_f4,
    }
    for s in range(2, 6):
        stages["N%d" % s] = lambda i, s=s: getattr(ns[i], "s%d" % s)()
        stages["C%d" % s] = lambda i, s=s: getattr(cs[i], "s%d" % s)()
    for s in range(2, 5):
        stages["g%d" % s] = lambda i, s=s: getattr(gs[i], "s%d" % s)()
    for name, i in ORDER:
        stages[name](i)
    copy.finish()
    assert len(copy.all) <= MAX_COPIES


def merger_call(cnt, own, st, gain, bias, gs, feat, win, wout):
    vm = pl.BlockSpec(memory_space=pltpu.VMEM)
    hb = pl.BlockSpec(memory_space=pl.ANY)
    na, nb = G_KINDS.count("A") * GW, G_KINDS.count("B") * GW
    buf = lambda *shape: pltpu.VMEM(shape, BF)
    return pl.pallas_call(
        merger_kernel,
        out_shape=(
            jax.ShapeDtypeStruct((SLOTS, MW), BF),
            jax.ShapeDtypeStruct((320, HID), BF),
            jax.ShapeDtypeStruct((HID, BW), BF),
        ),
        in_specs=[vm, vm, vm, vm, vm, hb, hb, hb, hb],
        out_specs=(vm, vm, vm),
        scratch_shapes=[
            buf(SLOTS, TOK),
            buf(4 * SLOTS, 4 * SLOTS),
            buf(4, 2, SLOTS, D),
            buf(SLOTS, MW),
            buf(MW, HID),
            buf(16, HID, BW),
            buf(4, SLOTS, D),
            buf(2, SLOTS, D),
            buf(SLOTS, D),
            buf(8, SLOTS, D),
            buf(8, SLOTS, MW),
            pltpu.VMEM((ROWS, HID), F32),
            pltpu.VMEM((ROWS, HID), F32),
            buf(HID, ROWS),
            buf(ROWS, HID),
            buf(2, 4, HID, BW),
            buf(4, 4, HH, BW),
            buf(4, 2, HH // 2, BW),
            buf(4, 2, HH, BW),
            buf(4, HH, BW),
            buf(2, HH, BW),
            buf(HH, BW),
            buf(2, 2, HALF, na),
            buf(2, 2, SLOTS, na),
            buf(SLOTS, na),
            buf(2, 1, HALF, nb),
            buf(2, 1, SLOTS, nb),
            buf(4, SLOTS, nb),
            pltpu.VMEM((SLOTS, MW), F32),
            buf(4, 2, 320, HID),
            buf(2, 2, 160, HID),
            buf(2, 2, 320, HID),
            buf(320, HID),
            pltpu.SemaphoreType.DMA((MAX_COPIES,)),
            pltpu.SemaphoreType.DMA((MAX_COPIES,)),
            pltpu.SemaphoreType.DMA((40,)),
        ],
        compiler_params=pltpu.CompilerParams(
            collective_id=0, has_side_effects=True, vmem_limit_bytes=63 * 2**20
        ),
        cost_estimate=pl.CostEstimate(
            flops=2 * 512 * 384 * 31744, bytes_accessed=16 * 2**20, transcendentals=400000
        ),
        name="merger_backward",
    )(cnt, own, st, gain, bias, gs, feat, win, wout)


def local(
    grad_seq, features, merger_norm_gain, w_in, b_in, w_out, image_counts, sample_owner, image_starts
):
    mig, gw1, gw2 = merger_call(
        image_counts, sample_owner, image_starts, merger_norm_gain, b_in,
        grad_seq.reshape(2, 2, SLOTS, D), features[0], w_in, w_out,
    )
    return (mig[None], gw1, gw2)


def solution(mesh):
    in_specs = (
        P("dp", "seq", None),
        P("dp", "seq", None),
        P(),
        P(None, "dp"),
        P("dp"),
        P("dp", None),
        P("dp", None),
        P("dp", None),
        P("dp", None),
    )
    out_specs = (P("dp", "seq", None), P("seq", "dp"), P("dp", "seq"))
    return jax.shard_map(local, mesh=mesh, in_specs=in_specs, out_specs=out_specs, check_vma=False)
```

time: 558 us -> 153 us (0.27)
  waiting for transfers between devices: 460 us -> 0 us
  Pallas kernels: 0 us -> 146 us
  matrix products: 39.6 us -> 0 us
  local copies, waits for them, and re-layouts: 24.4 us -> 5.39 us
  other arithmetic: 15.8 us -> 0 us
  between operations: 14.3 us -> 0.64 us
    all_gather x3 -> x0, waiting for transfers between devices: 260 us -> none  [the longest x1 102 us: local(): piece = lax.all_gather(returned, 'dp', axis=0, tiled=True)]
    reduce_scatter x3 -> x0, waiting for transfers between devices: 200 us -> none  [the longest x1 72.5 us: local(): lax.psum_scatter(weight_total.astype(jnp.bfloat16), 'seq', scatter_dimens...]
    pallas_call x0 -> x1, Pallas kernels: none -> 146 us  [merger_call(): pl.pallas_call(merger_kernel, out_shape=(jax.ShapeDtypeStruct((SLOTS, MW)...]
    dot_general x5 -> x0, matrix products: 39.6 us -> none  [the longest x1 10.1 us: local(): lax.dot_general(piece, w_out, (((1,), (1,)), ((), ())), preferred_element...]
    gather x2 -> x0, local copies, waits for them, and re-layouts: 16 us -> none  [the longest x1 11.1 us: return_gradients(): jnp.take(everything, index, axis=0)]
  transfers between devices with their start and end apart: 6 -> 0, of which waited for: 6 -> 0; matrix products, arithmetic and copies ran while one was open for 9% -> 0% of each run, Pallas kernels for 0% -> 0%
where the time goes in v2:
time: 153 us; the launch traced here: 152 us
  Pallas kernels  146 us (95%)
  local copies, waits for them, and re-layouts  5.39 us (4%)
    pallas_call x1, Pallas kernels, merger_call(): pl.pallas_call(merger_kernel, out_shape=(jax.ShapeDtypeStruct((SLOTS, MW)...  146 us
    unnamed x3, local copies, waits for them, and re-layouts  5.39 us

profile of v2, /device:TPU:1, one launch (start us, length us, event | category | flops | bytes accessed | tf_op | source)
XLA Modules:
  0.0 152.5 jit_solution(17387101319179708423)
XLA Ops:
  0.6 146.4 %merger_backward.1 = (bf16[64,5120]{1,0:T(8,128)(2,1)}, bf16[320,384]{1,0:T(8,128)(2,1)}, bf16[384,512]{1,0:T(8,128)(2,1)}) custom-call(s32[1,64]{1,0:T(1,128)} %cnt_ref.1, s32[1,64]{1,0:T(1,128)} %own_ref.1, s32[1,64]{1,0:T(1,128)} %st_ref.1, f32[1280]{0:T(1024)} %gain_ref.1, f32[384]{0:T(512)} %b_ref.1, bf16[2,2,64,8192]{3,2,1,0:T(8,128)(2,1)} %bitcast.4, ...), custom_call_target="tpu_custom_call" | custom-call | flops 12482248704 | bytes 16777216 | tf_op jit(solution)/shard_map/merger_backward/pallas_call | solution.py:574
  147.1 2.0 %copy.15 = bf16[1,64,5120]{2,1,0:T(8,128)(2,1)} copy(bf16[1,64,5120]{2,1,0:T(8,128)(2,1)} %bitcast.3) | data formatting | bytes 1310720
  149.0 1.7 %copy.16 = bf16[320,384]{1,0:T(8,128)(2,1)} copy(bf16[320,384]{1,0:T(8,128)(2,1)} %get-tuple-element.13) | data formatting | bytes 491520
  150.7 1.8 %copy.17 = bf16[384,512]{1,0:T(8,128)(2,1)} copy(bf16[384,512]{1,0:T(8,128)(2,1)} %get-tuple-element.14) | data formatting | bytes 786432

commit v3 on v2

v3 whole, which is shorter than its diff:
```python
import jax
import jax.numpy as jnp
from jax import lax
from jax.experimental import pallas as pl
from jax.experimental.pallas import tpu as pltpu
from jax.sharding import PartitionSpec as P

EPS = 1e-06
MESH = pl.DeviceIdType.MESH
BF = jnp.bfloat16
F32 = jnp.float32
I32 = jnp.int32
D = 8192
MW = 5120
VW = 1280
HID = 384
HH = HID // 2
SLOTS = 64
TOK = 256
ROWS = 512
HALF = 32
BW = 512
CW = 1024
KW = 2048
RB = 32
NT_DIMS = (((1,), (1,)), ((), ()))
TN_DIMS = (((0,), (0,)), ((), ()))
N_KINDS = "ABAB"
C_KINDS = "AABAABAB"
ORDER = (
    ("wi1", 0), ("norm", 0), ("norm", 1), ("pack", 0), ("pack", 1), ("ring", 0), ("norm", 2), ("pack", 2),
    ("ring", 1), ("pack", 3), ("norm", 3), ("route", 0), ("wi2", 0), ("ring", 2), ("N2", 0), ("route", 1),
    ("across", 0), ("N2", 3), ("pack", 4), ("N3", 2), ("ring", 3), ("route", 2), ("N2", 2), ("across", 1),
    ("ring", 4), ("across", 2), ("N2", 1), ("N3", 0), ("arrive", 0), ("pack", 5), ("N4", 2), ("N4", 0),
    ("route", 3), ("route", 4), ("across", 3), ("pack", 6), ("arrive", 2), ("arrive", 1), ("C1", 0),
    ("pack", 7), ("across", 4), ("C1", 4), ("N3", 3), ("arrive", 3), ("N5", 0), ("C1", 1), ("C1", 5),
    ("ring", 6), ("C2", 4), ("N5", 2), ("ring", 5), ("route", 6), ("N3", 1), ("ring", 7), ("C3", 4),
    ("C2", 5), ("route", 7), ("C2", 0), ("wi3", 0), ("route", 5), ("C3", 0), ("C4", 4), ("C3", 5),
    ("pre", 2), ("across", 5), ("across", 7), ("arrive", 4), ("C4", 0), ("C2", 1), ("arrive", 5), ("N5", 1),
    ("C1", 2), ("arrive", 7), ("C1", 6), ("N5", 3), ("C3", 1), ("across", 6), ("C5", 4), ("C5", 0),
    ("pre", 1), ("wi4", 0), ("C4", 1), ("pre", 0), ("C5", 5), ("pre", 3), ("C2", 2), ("arrive", 6),
    ("act", 0), ("C1", 3), ("w2", 0), ("C1", 7), ("w2a", 0), ("C5", 1), ("C3", 2), ("w2", 1), ("hid", 0),
    ("C2", 6), ("w2a", 1), ("wi5", 0), ("C2", 7), ("w2b", 0), ("C2", 3), ("hid", 5), ("C3", 6), ("w2b", 1),
    ("hid", 1), ("C4", 6), ("hid", 4), ("C3", 7), ("C4", 3), ("C5", 2), ("w2c", 0), ("C3", 3), ("hid", 2),
    ("C5", 6), ("w2", 2), ("hid", 6), ("w2c", 1), ("C5", 3), ("hid", 3), ("w2a", 2), ("C5", 7), ("w2", 3),
    ("gp", 0), ("hid", 7), ("w2a", 3), ("gp", 1), ("g1", 2), ("w2b", 2), ("w2z", 0), ("g1", 1), ("gy", 0),
    ("gn", 3), ("v0", 2), ("gn", 0), ("f1", 0), ("gn", 2), ("g1", 3), ("g1", 0), ("g2", 3), ("v0", 1),
    ("gy", 1), ("gn", 7), ("w2b", 3), ("w2c", 2), ("gn", 1), ("v0", 3), ("v0", 0), ("e1", 0), ("gn", 6),
    ("gn", 5), ("g2", 0), ("w2s", 0), ("f2", 0), ("g2", 1), ("w2c", 3), ("g2", 6), ("gn", 4), ("g3", 3),
    ("g2", 5), ("g2", 2), ("w2z", 1), ("g3", 0), ("g3", 1), ("e2", 0), ("g2", 7), ("g2", 4), ("f3", 0),
    ("e3", 0), ("g3", 6), ("w2s", 1), ("w2o", 0), ("g3", 2), ("w2f", 0), ("g3", 7), ("g3", 5), ("e4", 0),
    ("g3", 4), ("f4", 0),
)
MAX_COPIES = 256


def normal_cdf(value):
    return 0.5 * (1.0 + lax.erf(value * 0.7071067811865476))


def normal_pdf(value):
    return jnp.exp(-0.5 * value * value) * 0.3989422804014327


def dot(a, b):
    return jnp.dot(a, b, preferred_element_type=F32)


class Place:
    def __init__(self):
        d = lax.axis_index("dp")
        s = lax.axis_index("seq")
        self.seq = s
        self.x, self.zh = lax.div(d, 2), lax.rem(d, 2)
        self.zl, self.y, self.c = lax.div(s, 8), lax.rem(lax.div(s, 2), 4), lax.rem(s, 2)
        self.XP = self.dev(x=self.xs(1))
        self.XM = self.dev(x=self.xs(3))
        self.YP = self.dev(y=self.ys(1))
        self.YM = self.dev(y=self.ys(3))
        self.ZX = self.dev(zh=1 - self.zh, zl=1 - self.zl)
        self.ZL = self.dev(zl=1 - self.zl)
        self.CO = self.dev(c=1 - self.c)

    def xs(self, k):
        return lax.rem(self.x + k, 4)

    def ys(self, k):
        return lax.rem(self.y + k, 4)

    def dev(self, **kw):
        g = lambda n: kw.get(n, getattr(self, n))
        return (g("x") * 2 + g("zh"), g("zl") * 8 + g("y") * 2 + g("c"))

    def greet(self):
        for to in (self.XP, self.XM, self.YP, self.YM, self.ZX, self.ZL, self.CO):
            pl.semaphore_signal(pltpu.get_barrier_semaphore(), inc=1, device_id=to, device_id_type=MESH)

    def meet(self):
        pl.semaphore_wait(pltpu.get_barrier_semaphore(), 7)


class Copies:
    def __init__(self, send, recv):
        self.send, self.recv, self.all, self.sent = send, recv, [], set()

    def __call__(self, src, dst, to):
        i = len(self.all)
        cp = pltpu.make_async_remote_copy(
            src_ref=src, dst_ref=dst, send_sem=self.send.at[i], recv_sem=self.recv.at[i],
            device_id=to, device_id_type=MESH,
        )
        cp.start()
        self.all.append(cp)
        return cp

    def leave(self, copies):
        for cp in copies:
            if id(cp) not in self.sent:
                self.sent.add(id(cp))
                cp.wait_send()

    def finish(self):
        self.leave(self.all)


class Gather:
    def __init__(self, pc, copy, buf, row, rows, lo, w, z_first):
        self.pc, self.copy, self.buf, self.z_first = pc, copy, buf, z_first
        self.rows, self.lo, self.w, self.r = pl.ds(row, rows), lo, w, []

    def blk(self, k, z, part=0, parts=1):
        w = self.w // parts
        return self.buf.at[self.pc.xs(k) * 2 + z, self.rows, pl.ds(self.lo + part * w, w)]

    def to(self, ref, where):
        return self.copy(ref, ref, where)

    def s1(self):
        pc = self.pc
        own = self.blk(0, pc.zh)
        if self.z_first:
            self.z = self.to(own, pc.ZX)
        self.p, self.m = self.to(own, pc.XP), self.to(own, pc.XM)
        if not self.z_first:
            self.z = self.to(own, pc.ZX)

    def relay(self, z):
        pc = self.pc
        return [self.to(self.blk(3, z, 0, 2), pc.XP), self.to(self.blk(1, z, 1, 2), pc.XM)]

    def s2(self):
        pc = self.pc
        if self.z_first:
            self.z.wait_recv()
            other = self.blk(0, 1 - pc.zh)
            self.zp, self.zm = self.to(other, pc.XP), self.to(other, pc.XM)
        else:
            self.p.wait_recv()
            self.m.wait_recv()
            self.r += self.relay(pc.zh)
            self.f = [self.to(self.blk(3, pc.zh), pc.ZX), self.to(self.blk(1, pc.zh), pc.ZX)]

    def s3(self):
        pc = self.pc
        if self.z_first:
            self.p.wait_recv()
            self.m.wait_recv()
            self.r += self.relay(pc.zh)
        else:
            for cp in self.r:
                cp.wait_recv()
            self.f.append(self.to(self.blk(2, pc.zh), pc.ZX))

    def s4(self):
        self.zp.wait_recv()
        self.zm.wait_recv()
        self.r += self.relay(1 - self.pc.zh)

    def s5(self):
        for cp in self.r if self.z_first else [self.z] + self.f:
            cp.wait_recv()


def routing_tables(pc, cnt, own, st):
    iota = lambda shape, axis: lax.broadcasted_iota(I32, shape, axis)
    one = lambda m: jnp.where(m, 1.0, 0.0).astype(BF)
    i0, i1 = iota((64, 64), 0), iota((64, 64), 1)
    col = lambda r: jnp.sum(jnp.where(i0 == i1, r, 0), axis=1, keepdims=True)
    sh = lax.div(st, TOK)
    cnt_c, own_c, st_c, sh_c = col(cnt), col(own), col(st), col(sh)
    before_o = jnp.sum(jnp.where((own_c == own) & (i0 < i1), cnt_c, 0), axis=0, keepdims=True)
    before_h = jnp.sum(jnp.where((sh_c == sh) & (i1 < i0), cnt, 0), axis=1, keepdims=True)
    off = iota((64, TOK), 1) + pc.seq * TOK - st_c
    inside = (sh_c == pc.seq) & (off >= 0) & (off < cnt_c)
    rank = jnp.sum(jnp.where(inside, before_h + off + 1, 0), axis=0, keepdims=True) - 1
    pack = one(iota((64, TOK), 0) == rank)
    r = iota((256, 64), 0)
    q, k = lax.div(r, 64), lax.rem(r, 64)
    core = pc.c + lax.div(q, 2) * (1 - 2 * pc.c)
    zl = pc.zl + lax.rem(q, 2) * (1 - 2 * pc.zl)
    off = k - before_o
    inside = (own == zl * 8 + pc.y * 2 + core) & (off >= 0) & (off < cnt)
    want = jnp.sum(jnp.where(inside, st + off + 1, 0), axis=1, keepdims=True)
    r = iota((64, 256), 1)
    off = lax.rem(r, 64) - before_h
    inside = (sh_c == pc.zl * 8 + lax.div(r, 64) * 2 + pc.c) & (off >= 0) & (off < cnt_c)
    held = jnp.sum(jnp.where(inside, st_c + off + 1, 0), axis=0, keepdims=True)
    return pack, one((want == held) & (want > 0))


def merger_kernel(
    cnt_ref, own_ref, st_ref, gain_ref, b_ref, gs_hbm, feat_hbm, win_hbm, wout_hbm,
    mig_ref, gw1_ref, gw2_ref,
    pack_m, route_m, big, feat, win, win2, wout, g, hc, hz, rt, nt, pre, gh, act_t, gp, gp2,
    w2, cr2, ya2, yb2, ss, zr2, o2, xa, xb, cr1, ya1, yb1, zr1, eb1, ec1, ed1,
    send, recv, lsem,
):
    pc = Place()
    copy = Copies(send, recv)
    me = pc.x * 2 + pc.zh
    nc = D // CW
    cut = lambda i: pl.ds(i * CW, CW)
    loads = []

    def load(src, dst):
        cp = pltpu.make_async_copy(src, dst, lsem.at[len(loads)])
        cp.start()
        loads.append(cp)
        return cp

    def piece(p):
        return pl.ds(((p // 4) % 2 * 8 + p % 4 * 2 + p // 8) * BW, BW)

    lf = load(feat_hbm, feat)
    lg = [load(gs_hbm.at[:, :, :, piece(p)], big.at[0:2, :, :, pl.ds(p * BW, BW)]) for p in range(16)]
    lw = load(win_hbm, win)
    lo = [load(wout_hbm.at[:, piece(p)], wout.at[p // 8, p // 4 % 2, p % 4]) for p in range(16)]
    pc.greet()
    pack_m[...], route_m[...] = routing_tables(pc, cnt_ref[...], own_ref[...], st_ref[...])
    gain = gain_ref[...].reshape(1, VW)
    pc.meet()

    yp, ym, rp, rm, co, zl = ({} for _ in range(6))

    def do_pack(i):
        lg[2 * i].wait()
        lg[2 * i + 1].wait()
        g[pc.y, :, cut(i)] = dot(pack_m[...], big[0:2, :, :, cut(i)].reshape(TOK, CW)).astype(BF)
        own = g.at[pc.y, :, cut(i)]
        yp[i] = copy(own, own, pc.YP)
        ym[i] = copy(own, own, pc.YM)

    def do_ring(i):
        yp[i].wait_recv()
        up = g.at[pc.ys(3), pl.ds(0, HALF), cut(i)]
        rp[i] = copy(up, up, pc.YP)
        ym[i].wait_recv()
        down = g.at[pc.ys(1), pl.ds(HALF, HALF), cut(i)]
        rm[i] = copy(down, down, pc.YM)

    def do_route(i):
        rp[i].wait_recv()
        rm[i].wait_recv()
        for j in range(CW // 512):
            cols = pl.ds(i * CW + j * 512, 512)
            big[2:4, :, :, cols] = (
                dot(route_m[...], g[:, :, cols].reshape(4 * SLOTS, 512)).astype(BF).reshape(2, 2, SLOTS, 512)
            )
        co[i] = copy(big.at[3, :, :, cut(i)], hc.at[:, :, cut(i)], pc.CO)

    def do_across(i):
        co[i].wait_recv()
        big[2, :, :, cut(i)] = big[2, :, :, cut(i)] + hc[:, :, cut(i)]
        zl[i] = copy(big.at[2, 1, :, cut(i)], hz.at[:, cut(i)], pc.ZL)

    cs = [Gather(pc, copy, rt, i // 4 * RB, RB, i % 4 * KW, KW, C_KINDS[i] == "A") for i in range(8)]
    ns = [Gather(pc, copy, nt, 0, SLOTS, n * VW, VW, N_KINDS[n] == "A") for n in range(4)]

    def do_arrive(i):
        zl[i].wait_recv()
        rt[me, :, cut(i)] = big[2, 0, :, cut(i)] + hz[:, cut(i)]

    def standardized(n, row=0, rows=SLOTS):
        v = feat[row:row + rows, n * VW:(n + 1) * VW].astype(F32)
        d = v - jnp.mean(v, axis=1, keepdims=True)
        inv = lax.rsqrt(jnp.mean(d * d, axis=1, keepdims=True) + EPS)
        return d * inv, inv

    def do_norm(n):
        if n == 0:
            lf.wait()
        nt[me, :, n * VW:(n + 1) * VW] = (standardized(n)[0] * gain).astype(BF)
        ns[n].s1()

    def do_pre(n):
        part = dot(
            nt[:, :, n * VW:(n + 1) * VW].reshape(ROWS, VW), win[n * VW:(n + 1) * VW, :]
        ).reshape(8, SLOTS, HID)
        if started:
            pre[...] += part
        else:
            pre[...] = part + b_ref[...].reshape(1, 1, HID)
            started.append(n)

    started = []

    def do_act(_):
        def tile(k, _):
            at = pl.ds(k * 2, 2)
            v = pre[at].reshape(128, HID)
            cdf = normal_cdf(v)
            act_t[:, pl.ds(pl.multiple_of(k * 128, 128), 128)] = (v * cdf).T.astype(BF)
            pre[at] = (cdf + v * normal_pdf(v)).reshape(2, SLOTS, HID)
            return 0

        lax.fori_loop(0, 4, tile, 0)

    opened = set()

    def do_hid(i):
        b, k = i // 4, i % 4
        part = None
        for y in range(4):
            p = 4 * k + y
            if p not in ready:
                lo[p].wait()
                ready.add(p)
            one = lax.dot_general(
                rt[:, b * RB:(b + 1) * RB, p * BW:(p + 1) * BW].reshape(8 * RB, BW),
                wout[k // 2, k % 2, y], NT_DIMS, preferred_element_type=F32,
            )
            part = one if part is None else part + one
        if b in opened:
            gh[b] += part
        else:
            gh[b] = part
            opened.add(b)

    ready = set()

    mine = pl.ds(pl.multiple_of(pc.c * HH, HH), HH)
    theirs = pl.ds(pl.multiple_of((1 - pc.c) * HH, HH), HH)
    wc, wa, wb, wz, wo = ({} for _ in range(5))

    def do_w2(k):
        b = k % 2
        if k >= 2:
            copy.leave([wc[k - 2]] + wa[k - 2] + wb[k - 2])

        def tile(y, _):
            cols = pl.ds(pl.multiple_of(k * 4 * BW + y * BW, BW), BW)
            w2[b, y] = dot(act_t[...], rt[:, :, cols].reshape(ROWS, BW)).astype(BF)
            return 0

        lax.fori_loop(0, 4, tile, 0)
        wc[k] = copy(w2.at[b, :, theirs], cr2.at[k], pc.CO)

    def do_w2a(k):
        b, y = k % 2, pc.ys(2)
        wc[k].wait_recv()
        w2[b, y, mine] = w2[b, y, mine] + cr2[k, y]
        wa[k] = []
        for d, to in enumerate((pc.YP, pc.YM)):
            rows = pl.ds(pl.multiple_of(pc.c * HH + d * HH // 2, HH // 2), HH // 2)
            wa[k].append(copy(w2.at[b, y, rows], ya2.at[k, d], to))

    def do_w2b(k):
        b = k % 2
        wb[k] = []
        for d, (r, to) in enumerate(((1, pc.YP), (3, pc.YM))):
            y = pc.ys(r)
            w2[b, y, mine] = w2[b, y, mine] + cr2[k, y]
            wa[k][d].wait_recv()
            rows = pl.ds(pl.multiple_of(pc.c * HH + d * HH // 2, HH // 2), HH // 2)
            w2[b, y, rows] = w2[b, y, rows] + ya2[k, d]
            wb[k].append(copy(w2.at[b, y, mine], yb2.at[k, d], to))

    def do_w2c(k):
        for cp in wb[k]:
            cp.wait_recv()
        ss[k] = (
            w2[k % 2, pc.y, mine].astype(F32) + cr2[k, pc.y].astype(F32)
            + yb2[k, 0].astype(F32) + yb2[k, 1].astype(F32)
        ).astype(BF)

    def do_w2z(q):
        wz[q] = copy(ss.at[1 - pc.zl + 2 * q], zr2.at[q], pc.ZL)

    def do_w2s(q):
        wz[q].wait_recv()
        ss[pc.zl + 2 * q] = ss[pc.zl + 2 * q] + zr2[q]

    def do_w2o(_):
        wo[0] = copy(ss.at[pc.zl + 2 * (1 - pc.c)], o2, pc.CO)

    def do_w2f(_):
        wo[0].wait_recv()
        gw2_ref[mine, :] = ss[pc.zl + 2 * pc.c]
        gw2_ref[theirs, :] = o2[...]

    gx, ga, gb, wi = {}, {}, {}, {}

    def share(z, n=1):
        return pl.ds(pl.multiple_of((pc.c * 8 + pc.y * 2 + z) * 320, 320), n * 320)

    def do_wi1(_):
        lw.wait()
        wi[1] = [copy(win.at[share(1 - pc.zl)], win2.at[share(1 - pc.zl)], pc.ZX)]

    def pass_on(n, refs):
        for cp in wi[n - 1]:
            cp.wait_recv()
        wi[n] = [copy(win2.at[rows], win2.at[rows], to) for rows, to in refs]

    def do_wi2(_):
        pass_on(2, [(share(pc.zl), pc.ZL)])

    def do_wi3(_):
        pass_on(3, [(share(0, 2), pc.YP), (share(0, 2), pc.YM)])

    def do_wi4(_):
        at = lambda k, z: pl.ds(pl.multiple_of((pc.c * 8 + pc.ys(k) * 2 + z) * 320, 320), 320)
        pass_on(4, [(at(3, 0), pc.YP), (at(1, 1), pc.YM)])

    def do_wi5(_):
        pass_on(5, [(pl.ds(pl.multiple_of(pc.c * 2560, 2560), 2560), pc.CO)])

    def do_gp(b):
        rows = pl.ds(b * RB, RB)
        gp[:, :, rows, :] = (
            (gh[b].reshape(8, RB, HID) * pre[:, rows, :]).astype(BF).reshape(4, 2, RB, HID)
        )
        copy.leave(list(co.values()) + list(zl.values()))
        gx[b] = copy(gp.at[:, 1 - pc.zh, rows], gp2.at[:, rows], pc.ZX)

    def do_gy(b):
        for cp in wi.pop(5, []):
            cp.wait_recv()
        gx[b].wait_recv()

    def do_gn(i):
        b, j = i // 4, i % 4
        rows, at = pl.ds(b * RB, RB), slice(j * VW, (j + 1) * VW)
        part = lax.dot_general(
            gp[:, pc.zh, rows, :].reshape(4 * RB, HID), win[at, :], NT_DIMS, preferred_element_type=F32
        ) + lax.dot_general(
            gp2[:, rows, :].reshape(4 * RB, HID), win2[at, :], NT_DIMS, preferred_element_type=F32
        )
        big[:, 0, rows, at] = part.astype(BF).reshape(4, RB, VW)
        ga[i] = [
            copy(
                big.at[pc.xs(2), 0, rows, pl.ds(j * VW + d * VW // 2, VW // 2)],
                xa.at[d, rows, pl.ds(j * VW // 2, VW // 2)], to,
            )
            for d, to in enumerate((pc.XP, pc.XM))
        ]

    def do_g2(i):
        b, j = i // 4, i % 4
        rows, at = pl.ds(b * RB, RB), pl.ds(j * VW, VW)
        gb[i] = []
        for d, (k, to) in enumerate(((1, pc.XP), (3, pc.XM))):
            ga[i][d].wait_recv()
            half = pl.ds(j * VW + d * VW // 2, VW // 2)
            near = pc.xs(k)
            big[near, 0, rows, half] = big[near, 0, rows, half] + xa[d, rows, pl.ds(j * VW // 2, VW // 2)]
            gb[i].append(copy(big.at[near, 0, rows, at], xb.at[d, rows, at], to))

    def do_g3(i):
        b, j = i // 4, i % 4
        rows, at = pl.ds(b * RB, RB), pl.ds(j * VW, VW)
        for cp in gb[i]:
            cp.wait_recv()
        total = (
            big[pc.x, 0, rows, at].astype(F32) + xb[0, rows, at].astype(F32) + xb[1, rows, at].astype(F32)
        )
        xhat, inv = standardized(j, b * RB, RB)
        t = total * gain
        mig_ref[rows, at] = (
            (t - jnp.mean(t, axis=1, keepdims=True) - xhat * jnp.mean(t * xhat, axis=1, keepdims=True)) * inv
        ).astype(BF)

    vc, va, vb, vz, ve, vf, vg = {}, [], [], [], [], [], []
    col_a, col_b = pl.ds(0, 256), pl.ds(256, 128)

    def w1(z, y, cols, row=0, rows=320):
        return wout.at[pc.c, z, y, pl.ds(row, rows), cols]

    def do_g1(k):
        y = pc.ys(k)

        def tile(z, _):
            cols = pl.ds(pl.multiple_of((z * 4 + y) * 640, 128), 640)
            part = lax.dot_general(
                nt[:, :, cols].reshape(ROWS, 640), gp[...].reshape(ROWS, HID), TN_DIMS,
                preferred_element_type=F32,
            ).astype(BF)
            wout[0, z, y, 0:320, 0:HID] = part[0:320]
            wout[1, z, y, 0:320, 0:HID] = part[320:640]
            return 0

        lax.fori_loop(0, 2, tile, 0)
        vc[k] = copy(wout.at[1 - pc.c, :, y, pl.ds(0, 320), pl.ds(0, HID)], cr1.at[:, y], pc.CO)

    def do_v0(k):
        y = pc.ys(k)
        vc[k].wait_recv()
        for z in range(2):
            part = w1(z, y, pl.ds(0, HID))
            part[...] = part[...] + cr1[z, y]

    def do_f1(_):
        for d, to in enumerate((pc.YP, pc.YM)):
            va.append(copy(w1(slice(None), pc.ys(2), col_a, d * 160, 160), ya1.at[d], to))

    def do_f2(_):
        for d, (r, to) in enumerate(((1, pc.YP), (3, pc.YM))):
            y = pc.ys(r)
            va[d].wait_recv()
            for z in range(2):
                part = w1(z, y, col_a, d * 160, 160)
                part[...] = part[...] + ya1[d, z]
            vb.append(copy(w1(slice(None), y, col_a), yb1.at[d], to))

    def total_a(z):
        return w1(z, pc.y, col_a)[...].astype(F32) + yb1[0, z].astype(F32) + yb1[1, z].astype(F32)

    def do_f3(_):
        for cp in vb:
            cp.wait_recv()
        there = w1(1 - pc.zl, pc.y, col_a)
        there[...] = total_a(1 - pc.zl).astype(BF)
        vz.append(copy(there, zr1, pc.ZL))

    def do_f4(_):
        vz[0].wait_recv()
        gw1_ref[:, 0:256] = (total_a(pc.zl) + zr1[...].astype(F32)).astype(BF)

    def do_e1(_):
        ve.append(copy(w1(1 - pc.zl, slice(None), col_b), eb1, pc.ZL))

    def do_e2(_):
        ve[0].wait_recv()
        for k in (2, 1, 3, 0):
            y = pc.ys(k)
            part = w1(pc.zl, y, col_b)
            part[...] = part[...] + eb1[y]
            if k == 2:
                for d, to in enumerate((pc.YP, pc.YM)):
                    vf.append(copy(w1(pc.zl, y, col_b, d * 160, 160), ec1.at[d], to))

    def do_e3(_):
        for d, (r, to) in enumerate(((1, pc.YP), (3, pc.YM))):
            y = pc.ys(r)
            vf[d].wait_recv()
            part = w1(pc.zl, y, col_b, d * 160, 160)
            part[...] = part[...] + ec1[d]
            vg.append(copy(w1(pc.zl, y, col_b), ed1.at[d], to))

    def do_e4(_):
        for cp in vg:
            cp.wait_recv()
        gw1_ref[:, 256:384] = (
            w1(pc.zl, pc.y, col_b)[...].astype(F32) + ed1[0].astype(F32) + ed1[1].astype(F32)
        ).astype(BF)

    stages = {
        "pack": do_pack, "ring": do_ring, "route": do_route, "across": do_across, "arrive": do_arrive,
        "norm": do_norm, "pre": do_pre, "act": do_act, "hid": do_hid, "gp": do_gp, "gy": do_gy, "gn": do_gn,
        "g2": do_g2, "g3": do_g3, "wi1": do_wi1, "wi2": do_wi2, "wi3": do_wi3, "wi4": do_wi4, "wi5": do_wi5,
        "w2": do_w2, "w2a": do_w2a, "w2b": do_w2b, "w2c": do_w2c, "w2z": do_w2z, "w2s": do_w2s,
        "w2o": do_w2o, "w2f": do_w2f, "g1": do_g1, "v0": do_v0, "f1": do_f1, "f2": do_f2, "f3": do_f3, "f4": do_f4,
        "e1": do_e1, "e2": do_e2, "e3": do_e3, "e4": do_e4,
    }
    for s in range(1, 6):
        stages["N%d" % s] = lambda i, s=s: getattr(ns[i], "s%d" % s)()
        stages["C%d" % s] = lambda i, s=s: getattr(cs[i], "s%d" % s)()
    for name, i in ORDER:
        stages[name](i)
    copy.finish()
    assert len(copy.all) <= MAX_COPIES


def merger_call(cnt, own, st, gain, bias, gs, feat, win, wout):
    vm = pl.BlockSpec(memory_space=pltpu.VMEM)
    hb = pl.BlockSpec(memory_space=pl.ANY)
    buf = lambda *shape: pltpu.VMEM(shape, BF)
    return pl.pallas_call(
        merger_kernel,
        out_shape=(
            jax.ShapeDtypeStruct((SLOTS, MW), BF),
            jax.ShapeDtypeStruct((320, HID), BF),
            jax.ShapeDtypeStruct((HID, BW), BF),
        ),
        in_specs=[vm, vm, vm, vm, vm, hb, hb, hb, hb],
        out_specs=(vm, vm, vm),
        scratch_shapes=[
            buf(SLOTS, TOK),
            buf(4 * SLOTS, 4 * SLOTS),
            buf(4, 2, SLOTS, D),
            buf(SLOTS, MW),
            buf(MW, HID),
            buf(MW, HID),
            buf(2, 2, 4, HID, BW),
            buf(4, SLOTS, D),
            buf(2, SLOTS, D),
            buf(SLOTS, D),
            buf(8, SLOTS, D),
            buf(8, SLOTS, MW),
            pltpu.VMEM((8, SLOTS, HID), F32),
            pltpu.VMEM((2, 8 * RB, HID), F32),
            buf(HID, ROWS),
            buf(4, 2, SLOTS, HID),
            buf(4, SLOTS, HID),
            buf(2, 4, HID, BW),
            buf(4, 4, HH, BW),
            buf(4, 2, HH // 2, BW),
            buf(4, 2, HH, BW),
            buf(4, HH, BW),
            buf(2, HH, BW),
            buf(HH, BW),
            buf(2, SLOTS, MW // 2),
            buf(2, SLOTS, MW),
            buf(2, 4, 320, HID),
            buf(2, 2, 160, 256),
            buf(2, 2, 320, 256),
            buf(320, 256),
            buf(4, 320, 128),
            buf(2, 160, 128),
            buf(2, 320, 128),
            pltpu.SemaphoreType.DMA((MAX_COPIES,)),
            pltpu.SemaphoreType.DMA((MAX_COPIES,)),
            pltpu.SemaphoreType.DMA((40,)),
        ],
        compiler_params=pltpu.CompilerParams(
            collective_id=0, has_side_effects=True, vmem_limit_bytes=63 * 2**20
        ),
        cost_estimate=pl.CostEstimate(
            flops=2 * 512 * 384 * 31744, bytes_accessed=16 * 2**20, transcendentals=400000
        ),
        name="merger_backward",
    )(cnt, own, st, gain, bias, gs, feat, win, wout)


def finish_kernel(a, b, c, ao, bo, co):
    for i, o in ((a, ao), (b, bo), (c, co)):
        o[...] = i[...]


def finish_call(*arrays):
    vm = pl.BlockSpec(memory_space=pltpu.VMEM)
    return pl.pallas_call(
        finish_kernel,
        out_shape=tuple(jax.ShapeDtypeStruct(a.shape, a.dtype) for a in arrays),
        in_specs=[vm] * 3,
        out_specs=(vm, vm, vm),
        compiler_params=pltpu.CompilerParams(vmem_limit_bytes=63 * 2**20),
        name="write_results",
    )(*arrays)


def local(
    grad_seq, features, merger_norm_gain, w_in, b_in, w_out, image_counts, sample_owner, image_starts
):
    mig, gw1, gw2 = merger_call(
        image_counts, sample_owner, image_starts, merger_norm_gain, b_in,
        grad_seq.reshape(2, 2, SLOTS, D), features[0], w_in, w_out,
    )
    mig, gw1, gw2 = finish_call(mig, gw1, gw2)
    return (mig[None], gw1, gw2)


def solution(mesh):
    in_specs = (
        P("dp", "seq", None),
        P("dp", "seq", None),
        P(),
        P(None, "dp"),
        P("dp"),
        P("dp", None),
        P("dp", None),
        P("dp", None),
        P("dp", None),
    )
    out_specs = (P("dp", "seq", None), P("seq", "dp"), P("dp", "seq"))
    return jax.shard_map(local, mesh=mesh, in_specs=in_specs, out_specs=out_specs, check_vma=False)
```

time: 153 us -> 143 us (0.935)
  local copies, waits for them, and re-layouts: 5.39 us -> 0 us
  Pallas kernels: 146 us -> 142 us
    pallas_call x1, Pallas kernels: 146 us -> 140 us  [merger_call(): pl.pallas_call(merger_kernel, out_shape=(jax.ShapeDtypeStruct((SLOTS, MW)...]
    unnamed x3 -> x0, local copies, waits for them, and re-layouts: 5.39 us -> none
    pallas_call x0 -> x1, Pallas kernels: none -> 2.39 us  [finish_call(): pl.pallas_call(finish_kernel, out_shape=tuple((jax.ShapeDtypeStruct(a.sha...]
where the time goes in v3:
time: 143 us
  Pallas kernels  142 us (99%)
    pallas_call x1, Pallas kernels, merger_call(): pl.pallas_call(merger_kernel, out_shape=(jax.ShapeDtypeStruct((SLOTS, MW)...  140 us

profile of v3, /device:TPU:1, one launch (start us, length us, event | category | flops | bytes accessed | tf_op | source)
XLA Modules:
  0.0 142.6 jit_solution(17804132845475495147)
XLA Ops:
  0.6 139.6 %merger_backward.1 = (bf16[64,5120]{1,0:T(8,128)(2,1)}, bf16[320,384]{1,0:T(8,128)(2,1)}, bf16[384,512]{1,0:T(8,128)(2,1)}) custom-call(s32[1,64]{1,0:T(1,128)} %cnt_ref.1, s32[1,64]{1,0:T(1,128)} %own_ref.1, s32[1,64]{1,0:T(1,128)} %st_ref.1, f32[1280]{0:T(1024)} %gain_ref.1, f32[384]{0:T(512)} %b_ref.1, bf16[2,2,64,8192]{3,2,1,0:T(8,128)(2,1)} %bitcast.3, ...), custom_call_target="tpu_custom_call" | custom-call | flops 12482248704 | bytes 16777216 | tf_op jit(solution)/shard_map/merger_backward/pallas_call | solution.py:588
  140.2 2.4 %write_results.1 = (bf16[64,5120]{1,0:T(8,128)(2,1)}, bf16[320,384]{1,0:T(8,128)(2,1)}, bf16[384,512]{1,0:T(8,128)(2,1)}) custom-call(bf16[64,5120]{1,0:T(8,128)(2,1)} %get-tuple-element.9.a, bf16[320,384]{1,0:T(8,128)(2,1)} %get-tuple-element.10.b, bf16[384,512]{1,0:T(8,128)(2,1)} %get-tuple-element.11.c), custom_call_target="tpu_custom_call" | custom-call | tf_op jit(solution)/shard_map/write_results/pallas_call | solution.py:652

commit v4 on v3

--- a/solution.py
+++ b/solution.py
@@ -28,28 +28,28 @@
 N_KINDS = "ABAB"
 C_KINDS = "AABAABAB"
 ORDER = (
-    ("wi1", 0), ("norm", 0), ("norm", 1), ("pack", 0), ("pack", 1), ("ring", 0), ("norm", 2), ("pack", 2),
-    ("ring", 1), ("pack", 3), ("norm", 3), ("route", 0), ("wi2", 0), ("ring", 2), ("N2", 0), ("route", 1),
-    ("across", 0), ("N2", 3), ("pack", 4), ("N3", 2), ("ring", 3), ("route", 2), ("N2", 2), ("across", 1),
-    ("ring", 4), ("across", 2), ("N2", 1), ("N3", 0), ("arrive", 0), ("pack", 5), ("N4", 2), ("N4", 0),
-    ("route", 3), ("route", 4), ("across", 3), ("pack", 6), ("arrive", 2), ("arrive", 1), ("C1", 0),
-    ("pack", 7), ("across", 4), ("C1", 4), ("N3", 3), ("arrive", 3), ("N5", 0), ("C1", 1), ("C1", 5),
-    ("ring", 6), ("C2", 4), ("N5", 2), ("ring", 5), ("route", 6), ("N3", 1), ("ring", 7), ("C3", 4),
-    ("C2", 5), ("route", 7), ("C2", 0), ("wi3", 0), ("route", 5), ("C3", 0), ("C4", 4), ("C3", 5),
-    ("pre", 2), ("across", 5), ("across", 7), ("arrive", 4), ("C4", 0), ("C2", 1), ("arrive", 5), ("N5", 1),
-    ("C1", 2), ("arrive", 7), ("C1", 6), ("N5", 3), ("C3", 1), ("across", 6), ("C5", 4), ("C5", 0),
-    ("pre", 1), ("wi4", 0), ("C4", 1), ("pre", 0), ("C5", 5), ("pre", 3), ("C2", 2), ("arrive", 6),
-    ("act", 0), ("C1", 3), ("w2", 0), ("C1", 7), ("w2a", 0), ("C5", 1), ("C3", 2), ("w2", 1), ("hid", 0),
-    ("C2", 6), ("w2a", 1), ("wi5", 0), ("C2", 7), ("w2b", 0), ("C2", 3), ("hid", 5), ("C3", 6), ("w2b", 1),
-    ("hid", 1), ("C4", 6), ("hid", 4), ("C3", 7), ("C4", 3), ("C5", 2), ("w2c", 0), ("C3", 3), ("hid", 2),
-    ("C5", 6), ("w2", 2), ("hid", 6), ("w2c", 1), ("C5", 3), ("hid", 3), ("w2a", 2), ("C5", 7), ("w2", 3),
-    ("gp", 0), ("hid", 7), ("w2a", 3), ("gp", 1), ("g1", 2), ("w2b", 2), ("w2z", 0), ("g1", 1), ("gy", 0),
-    ("gn", 3), ("v0", 2), ("gn", 0), ("f1", 0), ("gn", 2), ("g1", 3), ("g1", 0), ("g2", 3), ("v0", 1),
-    ("gy", 1), ("gn", 7), ("w2b", 3), ("w2c", 2), ("gn", 1), ("v0", 3), ("v0", 0), ("e1", 0), ("gn", 6),
-    ("gn", 5), ("g2", 0), ("w2s", 0), ("f2", 0), ("g2", 1), ("w2c", 3), ("g2", 6), ("gn", 4), ("g3", 3),
-    ("g2", 5), ("g2", 2), ("w2z", 1), ("g3", 0), ("g3", 1), ("e2", 0), ("g2", 7), ("g2", 4), ("f3", 0),
-    ("e3", 0), ("g3", 6), ("w2s", 1), ("w2o", 0), ("g3", 2), ("w2f", 0), ("g3", 7), ("g3", 5), ("e4", 0),
-    ("g3", 4), ("f4", 0),
+    ("norm", 0), ("pack", 0), ("pack", 1), ("pack", 2), ("norm", 1), ("norm", 2), ("N2", 1), ("N2", 0),
+    ("ring", 0), ("ring", 1), ("ring", 2), ("route", 0), ("N3", 0), ("pack", 3), ("norm", 3), ("across", 0),
+    ("pack", 4), ("pack", 5), ("route", 1), ("across", 1), ("route", 2), ("ring", 3), ("wi1", 0), ("N3", 2),
+    ("pack", 6), ("arrive", 0), ("across", 2), ("N2", 2), ("arrive", 1), ("C1", 0), ("ring", 5), ("ring", 4),
+    ("N4", 0), ("route", 3), ("N3", 1), ("across", 3), ("C1", 4), ("C2", 0), ("wi2", 0), ("pack", 7),
+    ("arrive", 2), ("ring", 6), ("arrive", 3), ("route", 5), ("N2", 3), ("C1", 1), ("C3", 4), ("across", 5),
+    ("N5", 1), ("ring", 7), ("N3", 3), ("C1", 5), ("route", 6), ("C2", 4), ("C4", 0), ("route", 7),
+    ("C3", 0), ("pre", 1), ("across", 6), ("route", 4), ("across", 7), ("wi3", 0), ("across", 4), ("C2", 5),
+    ("N5", 3), ("pre", 3), ("N4", 2), ("C2", 1), ("N5", 0), ("arrive", 7), ("arrive", 5), ("C3", 5),
+    ("arrive", 4), ("C4", 4), ("C3", 1), ("N5", 2), ("C1", 2), ("C5", 0), ("wi4", 0), ("pre", 0), ("pre", 2),
+    ("C1", 6), ("act", 0), ("C4", 1), ("C5", 4), ("w2", 0), ("C5", 5), ("w2a", 0), ("C2", 2), ("arrive", 6),
+    ("C1", 3), ("C5", 1), ("C2", 6), ("C3", 2), ("w2b", 0), ("C1", 7), ("C3", 6), ("w2", 1), ("hid", 5),
+    ("C4", 6), ("w2a", 1), ("wi5", 0), ("C2", 3), ("hid", 0), ("C2", 7), ("w2b", 1), ("w2c", 0), ("C5", 2),
+    ("C3", 3), ("C5", 6), ("w2", 2), ("hid", 4), ("C4", 3), ("hid", 1), ("w2a", 2), ("C3", 7), ("hid", 6),
+    ("w2c", 1), ("C5", 3), ("hid", 3), ("hid", 2), ("gp", 0), ("w2z", 0), ("w2b", 2), ("C5", 7), ("w2", 3),
+    ("hid", 7), ("gp", 1), ("g1", 2), ("gy", 0), ("w2a", 3), ("gn", 2), ("gn", 0), ("v0", 2), ("gn", 1),
+    ("f1", 0), ("g1", 1), ("f1", 1), ("g1", 3), ("g2", 2), ("g1", 0), ("w2b", 3), ("g2", 1), ("v0", 3),
+    ("v0", 1), ("gn", 3), ("v0", 0), ("gy", 1), ("e1", 0), ("gn", 4), ("f2", 1), ("gn", 7), ("gn", 5),
+    ("gn", 6), ("g3", 1), ("g3", 2), ("w2c", 2), ("g2", 0), ("g2", 3), ("w2c", 3), ("g2", 4), ("f2", 0),
+    ("w2z", 1), ("g2", 7), ("f3", 1), ("e2", 0), ("g3", 3), ("g2", 6), ("w2s", 0), ("g2", 5), ("f3", 0),
+    ("e3", 0), ("w2s", 1), ("g3", 7), ("w2o", 0), ("g3", 4), ("g3", 0), ("w2f", 0), ("f4", 1), ("g3", 6),
+    ("f4", 0), ("e4", 0), ("g3", 5),
 )
 MAX_COPIES = 256
 
@@ -293,6 +293,8 @@
         ns[n].s1()
 
     def do_pre(n):
+        if not started:
+            lw.wait()
         part = dot(
             nt[:, :, n * VW:(n + 1) * VW].reshape(ROWS, VW), win[n * VW:(n + 1) * VW, :]
         ).reshape(8, SLOTS, HID)
@@ -404,8 +406,7 @@
         return pl.ds(pl.multiple_of((pc.c * 8 + pc.y * 2 + z) * 320, 320), n * 320)
 
     def do_wi1(_):
-        lw.wait()
-        wi[1] = [copy(win.at[share(1 - pc.zl)], win2.at[share(1 - pc.zl)], pc.ZX)]
+        wi[1] = [copy(win_hbm.at[share(1 - pc.zl)], win2.at[share(1 - pc.zl)], pc.ZX)]
 
     def pass_on(n, refs):
         for cp in wi[n - 1]:
@@ -480,8 +481,8 @@
             (t - jnp.mean(t, axis=1, keepdims=True) - xhat * jnp.mean(t * xhat, axis=1, keepdims=True)) * inv
         ).astype(BF)
 
-    vc, va, vb, vz, ve, vf, vg = {}, [], [], [], [], [], []
-    col_a, col_b = pl.ds(0, 256), pl.ds(256, 128)
+    vc, va, vb, vz, ve, vf, vg = {}, {}, {}, {}, [], [], []
+    col_a, col_b = (pl.ds(0, 128), pl.ds(128, 128)), pl.ds(256, 128)
 
     def w1(z, y, cols, row=0, rows=320):
         return wout.at[pc.c, z, y, pl.ds(row, rows), cols]
@@ -509,32 +510,37 @@
             part = w1(z, y, pl.ds(0, HID))
             part[...] = part[...] + cr1[z, y]
 
-    def do_f1(_):
-        for d, to in enumerate((pc.YP, pc.YM)):
-            va.append(copy(w1(slice(None), pc.ys(2), col_a, d * 160, 160), ya1.at[d], to))
-
-    def do_f2(_):
+    def do_f1(p):
+        va[p] = [
+            copy(w1(slice(None), pc.ys(2), col_a[p], d * 160, 160), ya1.at[p, d], to)
+            for d, to in enumerate((pc.YP, pc.YM))
+        ]
+
+    def do_f2(p):
+        vb[p] = []
         for d, (r, to) in enumerate(((1, pc.YP), (3, pc.YM))):
             y = pc.ys(r)
-            va[d].wait_recv()
+            va[p][d].wait_recv()
             for z in range(2):
-                part = w1(z, y, col_a, d * 160, 160)
-                part[...] = part[...] + ya1[d, z]
-            vb.append(copy(w1(slice(None), y, col_a), yb1.at[d], to))
-
-    def total_a(z):
-        return w1(z, pc.y, col_a)[...].astype(F32) + yb1[0, z].astype(F32) + yb1[1, z].astype(F32)
-
-    def do_f3(_):
-        for cp in vb:
+                part = w1(z, y, col_a[p], d * 160, 160)
+                part[...] = part[...] + ya1[p, d, z]
+            vb[p].append(copy(w1(slice(None), y, col_a[p]), yb1.at[p, d], to))
+
+    def total_a(p, z):
+        return (
+            w1(z, pc.y, col_a[p])[...].astype(F32) + yb1[p, 0, z].astype(F32) + yb1[p, 1, z].astype(F32)
+        )
+
+    def do_f3(p):
+        for cp in vb[p]:
             cp.wait_recv()
-        there = w1(1 - pc.zl, pc.y, col_a)
-        there[...] = total_a(1 - pc.zl).astype(BF)
-        vz.append(copy(there, zr1, pc.ZL))
-
-    def do_f4(_):
-        vz[0].wait_recv()
-        gw1_ref[:, 0:256] = (total_a(pc.zl) + zr1[...].astype(F32)).astype(BF)
+        there = w1(1 - pc.zl, pc.y, col_a[p])
+        there[...] = total_a(p, 1 - pc.zl).astype(BF)
+        vz[p] = copy(there, zr1.at[p], pc.ZL)
+
+    def do_f4(p):
+        vz[p].wait_recv()
+        gw1_ref[:, p * 128:(p + 1) * 128] = (total_a(p, pc.zl) + zr1[p].astype(F32)).astype(BF)
 
     def do_e1(_):
         ve.append(copy(w1(1 - pc.zl, slice(None), col_b), eb1, pc.ZL))
@@ -622,9 +628,9 @@
             buf(2, SLOTS, MW // 2),
             buf(2, SLOTS, MW),
             buf(2, 4, 320, HID),
-            buf(2, 2, 160, 256),
-            buf(2, 2, 320, 256),
-            buf(320, 256),
+            buf(2, 2, 2, 160, 128),
+            buf(2, 2, 2, 320, 128),
+            buf(2, 320, 128),
             buf(4, 320, 128),
             buf(2, 160, 128),
             buf(2, 320, 128),

time: 143 us -> 138 us (0.965)
  Pallas kernels: 142 us -> 137 us
    pallas_call x1, Pallas kernels: 140 us -> 135 us  [merger_call(): pl.pallas_call(merger_kernel, out_shape=(jax.ShapeDtypeStruct((SLOTS, MW)...]
where the time goes in v4:
time: 138 us
  Pallas kernels  137 us (99%)
    pallas_call x1, Pallas kernels, merger_call(): pl.pallas_call(merger_kernel, out_shape=(jax.ShapeDtypeStruct((SLOTS, MW)...  135 us

profile of v4, /device:TPU:1, one launch (start us, length us, event | category | flops | bytes accessed | tf_op | source)
XLA Modules:
  0.0 137.9 jit_solution(12960455114377642252)
XLA Ops:
  0.6 134.9 %merger_backward.1 = (bf16[64,5120]{1,0:T(8,128)(2,1)}, bf16[320,384]{1,0:T(8,128)(2,1)}, bf16[384,512]{1,0:T(8,128)(2,1)}) custom-call(s32[1,64]{1,0:T(1,128)} %cnt_ref.1, s32[1,64]{1,0:T(1,128)} %own_ref.1, s32[1,64]{1,0:T(1,128)} %st_ref.1, f32[1280]{0:T(1024)} %gain_ref.1, f32[384]{0:T(512)} %b_ref.1, bf16[2,2,64,8192]{3,2,1,0:T(8,128)(2,1)} %bitcast.3, ...), custom_call_target="tpu_custom_call" | custom-call | flops 12482248704 | bytes 16777216 | tf_op jit(solution)/shard_map/merger_backward/pallas_call | solution.py:594
  135.5 2.4 %write_results.1 = (bf16[64,5120]{1,0:T(8,128)(2,1)}, bf16[320,384]{1,0:T(8,128)(2,1)}, bf16[384,512]{1,0:T(8,128)(2,1)}) custom-call(bf16[64,5120]{1,0:T(8,128)(2,1)} %get-tuple-element.9.a, bf16[320,384]{1,0:T(8,128)(2,1)} %get-tuple-element.10.b, bf16[384,512]{1,0:T(8,128)(2,1)} %get-tuple-element.11.c), custom_call_target="tpu_custom_call" | custom-call | tf_op jit(solution)/shard_map/write_results/pallas_call | solution.py:658

commit v5 on v4

--- a/solution.py
+++ b/solution.py
@@ -21,35 +21,40 @@
 HALF = 32
 BW = 512
 CW = 1024
-KW = 2048
+UW = BW // 2
+CA = 128
 RB = 32
 NT_DIMS = (((1,), (1,)), ((), ()))
 TN_DIMS = (((0,), (0,)), ((), ()))
 N_KINDS = "ABAB"
-C_KINDS = "AABAABAB"
+C_KINDS = ("AABA", "ABABA")
+CHUNKS = (((0, 2), (2, 2), (4, 2), (6, 2)), ((0, 2), (2, 2), (4, 2), (6, 1), (7, 1)))
+W2_UNITS = ((0, 2), (2, 2), (4, 2), (6, 1), (7, 1))
 ORDER = (
-    ("norm", 0), ("pack", 0), ("pack", 1), ("pack", 2), ("norm", 1), ("norm", 2), ("N2", 1), ("N2", 0),
-    ("ring", 0), ("ring", 1), ("ring", 2), ("route", 0), ("N3", 0), ("pack", 3), ("norm", 3), ("across", 0),
-    ("pack", 4), ("pack", 5), ("route", 1), ("across", 1), ("route", 2), ("ring", 3), ("wi1", 0), ("N3", 2),
-    ("pack", 6), ("arrive", 0), ("across", 2), ("N2", 2), ("arrive", 1), ("C1", 0), ("ring", 5), ("ring", 4),
-    ("N4", 0), ("route", 3), ("N3", 1), ("across", 3), ("C1", 4), ("C2", 0), ("wi2", 0), ("pack", 7),
-    ("arrive", 2), ("ring", 6), ("arrive", 3), ("route", 5), ("N2", 3), ("C1", 1), ("C3", 4), ("across", 5),
-    ("N5", 1), ("ring", 7), ("N3", 3), ("C1", 5), ("route", 6), ("C2", 4), ("C4", 0), ("route", 7),
-    ("C3", 0), ("pre", 1), ("across", 6), ("route", 4), ("across", 7), ("wi3", 0), ("across", 4), ("C2", 5),
-    ("N5", 3), ("pre", 3), ("N4", 2), ("C2", 1), ("N5", 0), ("arrive", 7), ("arrive", 5), ("C3", 5),
-    ("arrive", 4), ("C4", 4), ("C3", 1), ("N5", 2), ("C1", 2), ("C5", 0), ("wi4", 0), ("pre", 0), ("pre", 2),
-    ("C1", 6), ("act", 0), ("C4", 1), ("C5", 4), ("w2", 0), ("C5", 5), ("w2a", 0), ("C2", 2), ("arrive", 6),
-    ("C1", 3), ("C5", 1), ("C2", 6), ("C3", 2), ("w2b", 0), ("C1", 7), ("C3", 6), ("w2", 1), ("hid", 5),
-    ("C4", 6), ("w2a", 1), ("wi5", 0), ("C2", 3), ("hid", 0), ("C2", 7), ("w2b", 1), ("w2c", 0), ("C5", 2),
-    ("C3", 3), ("C5", 6), ("w2", 2), ("hid", 4), ("C4", 3), ("hid", 1), ("w2a", 2), ("C3", 7), ("hid", 6),
-    ("w2c", 1), ("C5", 3), ("hid", 3), ("hid", 2), ("gp", 0), ("w2z", 0), ("w2b", 2), ("C5", 7), ("w2", 3),
-    ("hid", 7), ("gp", 1), ("g1", 2), ("gy", 0), ("w2a", 3), ("gn", 2), ("gn", 0), ("v0", 2), ("gn", 1),
-    ("f1", 0), ("g1", 1), ("f1", 1), ("g1", 3), ("g2", 2), ("g1", 0), ("w2b", 3), ("g2", 1), ("v0", 3),
-    ("v0", 1), ("gn", 3), ("v0", 0), ("gy", 1), ("e1", 0), ("gn", 4), ("f2", 1), ("gn", 7), ("gn", 5),
-    ("gn", 6), ("g3", 1), ("g3", 2), ("w2c", 2), ("g2", 0), ("g2", 3), ("w2c", 3), ("g2", 4), ("f2", 0),
-    ("w2z", 1), ("g2", 7), ("f3", 1), ("e2", 0), ("g3", 3), ("g2", 6), ("w2s", 0), ("g2", 5), ("f3", 0),
-    ("e3", 0), ("w2s", 1), ("g3", 7), ("w2o", 0), ("g3", 4), ("g3", 0), ("w2f", 0), ("f4", 1), ("g3", 6),
-    ("f4", 0), ("e4", 0), ("g3", 5),
+    ("norm", 0), ("pack", 0), ("pack", 1), ("norm", 1), ("norm", 2), ("ring", 1), ("ring", 0), ("pack", 2),
+    ("pack", 3), ("N2", 1), ("pack", 4), ("N2", 0), ("route", 0), ("N2", 2), ("wi1", 0), ("across", 0),
+    ("N3", 2), ("ring", 2), ("N3", 0), ("ring", 3), ("norm", 3), ("N3", 1), ("route", 1), ("arrive", 0),
+    ("pack", 5), ("pack", 6), ("N4", 0), ("across", 1), ("N4", 2), ("arrive", 1), ("route", 3), ("wi2", 0),
+    ("ring", 4), ("C1", 0), ("ring", 6), ("ring", 5), ("across", 3), ("C1", 10), ("route", 2), ("N2", 3),
+    ("across", 2), ("N5", 1), ("pack", 7), ("C2", 0), ("route", 4), ("wi3", 0), ("N5", 0), ("C2", 10),
+    ("across", 4), ("N3", 3), ("ring", 7), ("route", 6), ("arrive", 3), ("route", 5), ("arrive", 2),
+    ("across", 5), ("C1", 11), ("C4", 10), ("C3", 0), ("across", 6), ("C4", 0), ("C1", 1), ("N5", 3),
+    ("arrive", 4), ("arrive", 5), ("arrive", 6), ("C1", 2), ("C2", 11), ("route", 7), ("C3", 10), ("pre", 1),
+    ("wi4", 0), ("pre", 3), ("pre", 0), ("N5", 2), ("pre", 2), ("C5", 0), ("C2", 1), ("C1", 12), ("hid", 0),
+    ("C3", 1), ("act", 0), ("across", 7), ("C5", 10), ("hid", 10), ("C3", 11), ("C4", 1), ("w2", 0),
+    ("arrive", 7), ("C1", 13), ("C2", 12), ("wi5", 0), ("C2", 2), ("C5", 11), ("C3", 12), ("C1", 14),
+    ("w2a", 0), ("C5", 1), ("w2", 1), ("C1", 3), ("w2a", 1), ("w2b", 0), ("C3", 2), ("C4", 12), ("C2", 14),
+    ("C2", 13), ("C2", 3), ("w2b", 1), ("C3", 14), ("C5", 12), ("w2c", 0), ("C5", 2), ("w2", 2), ("C4", 14),
+    ("C3", 3), ("C3", 13), ("hid", 2), ("hid", 12), ("w2a", 2), ("C4", 3), ("w2c", 1), ("hid", 11),
+    ("C5", 13), ("hid", 13), ("w2z", 0), ("C5", 14), ("hid", 14), ("gp", 1), ("hid", 1), ("w2b", 2),
+    ("C5", 3), ("hid", 3), ("gp", 0), ("g1", 2), ("w2", 3), ("gy", 1), ("gn", 6), ("gn", 5), ("v0", 2),
+    ("gn", 7), ("e1", 2), ("gn", 4), ("g1", 1), ("g2", 6), ("w2a", 3), ("f1", 0), ("w2c", 2), ("w2", 4),
+    ("g2", 5), ("v0", 1), ("e1", 1), ("g2", 7), ("g1", 3), ("w2a", 4), ("gy", 0), ("gn", 1), ("g2", 4),
+    ("e2", 2), ("w2s", 0), ("v0", 3), ("e1", 3), ("w2b", 3), ("g1", 0), ("gn", 3), ("w2b", 4), ("v0", 0),
+    ("e1", 0), ("gn", 0), ("gn", 2), ("f2", 0), ("g2", 1), ("w2c", 3), ("g3", 6), ("g3", 5), ("w2z", 1),
+    ("e2", 1), ("g3", 7), ("g2", 3), ("w2c", 4), ("e2", 3), ("w2z", 2), ("g2", 2), ("g2", 0), ("e3", 0),
+    ("g3", 1), ("g3", 4), ("e2", 0), ("f3", 0), ("w2s", 1), ("g3", 2), ("g3", 3), ("w2s", 2), ("w2o", 0),
+    ("e4", 0), ("g3", 0), ("w2f", 0), ("f4", 0),
 )
 MAX_COPIES = 256
 
@@ -229,22 +234,26 @@
         return cp
 
     def piece(p):
-        return pl.ds(((p // 4) % 2 * 8 + p % 4 * 2 + p // 8) * BW, BW)
-
+        return pl.ds(((p // 8) % 2 * 8 + p % 4 * 2 + p // 16) * BW + (p // 4) % 2 * UW, UW)
+
+    pc.greet()
     lf = load(feat_hbm, feat)
-    lg = [load(gs_hbm.at[:, :, :, piece(p)], big.at[0:2, :, :, pl.ds(p * BW, BW)]) for p in range(16)]
+    lg = [load(gs_hbm.at[:, :, :, piece(p)], big.at[0:2, :, :, pl.ds(p * UW, UW)]) for p in range(32)]
+    gain = gain_ref[...].reshape(1, VW)
+    pack_m[...], route_m[...] = routing_tables(pc, cnt_ref[...], own_ref[...], st_ref[...])
+    lf.wait()
     lw = load(win_hbm, win)
-    lo = [load(wout_hbm.at[:, piece(p)], wout.at[p // 8, p // 4 % 2, p % 4]) for p in range(16)]
-    pc.greet()
-    pack_m[...], route_m[...] = routing_tables(pc, cnt_ref[...], own_ref[...], st_ref[...])
-    gain = gain_ref[...].reshape(1, VW)
+    lo = [
+        load(wout_hbm.at[:, piece(p)], wout.at[p // 16, p // 8 % 2, p // 2 % 4, :, pl.ds(p % 2 * UW, UW)])
+        for p in range(32)
+    ]
     pc.meet()
 
     yp, ym, rp, rm, co, zl = ({} for _ in range(6))
 
     def do_pack(i):
-        lg[2 * i].wait()
-        lg[2 * i + 1].wait()
+        for p in range(4 * i, 4 * i + 4):
+            lg[p].wait()
         g[pc.y, :, cut(i)] = dot(pack_m[...], big[0:2, :, :, cut(i)].reshape(TOK, CW)).astype(BF)
         own = g.at[pc.y, :, cut(i)]
         yp[i] = copy(own, own, pc.YP)
@@ -273,7 +282,10 @@
         big[2, :, :, cut(i)] = big[2, :, :, cut(i)] + hc[:, :, cut(i)]
         zl[i] = copy(big.at[2, 1, :, cut(i)], hz.at[:, cut(i)], pc.ZL)
 
-    cs = [Gather(pc, copy, rt, i // 4 * RB, RB, i % 4 * KW, KW, C_KINDS[i] == "A") for i in range(8)]
+    cs = {
+        b * 10 + k: Gather(pc, copy, rt, b * RB, RB, u * CW, n * CW, C_KINDS[b][k] == "A")
+        for b in range(2) for k, (u, n) in enumerate(CHUNKS[b])
+    }
     ns = [Gather(pc, copy, nt, 0, SLOTS, n * VW, VW, N_KINDS[n] == "A") for n in range(4)]
 
     def do_arrive(i):
@@ -287,8 +299,6 @@
         return d * inv, inv
 
     def do_norm(n):
-        if n == 0:
-            lf.wait()
         nt[me, :, n * VW:(n + 1) * VW] = (standardized(n)[0] * gain).astype(BF)
         ns[n].s1()
 
@@ -320,16 +330,17 @@
     opened = set()
 
     def do_hid(i):
-        b, k = i // 4, i % 4
+        b = i // 10
+        u, n = CHUNKS[b][i % 10]
         part = None
-        for y in range(4):
-            p = 4 * k + y
-            if p not in ready:
-                lo[p].wait()
-                ready.add(p)
+        for q in range(2 * u, 2 * (u + n)):
+            for p in (2 * q, 2 * q + 1):
+                if p not in ready:
+                    lo[p].wait()
+                    ready.add(p)
             one = lax.dot_general(
-                rt[:, b * RB:(b + 1) * RB, p * BW:(p + 1) * BW].reshape(8 * RB, BW),
-                wout[k // 2, k % 2, y], NT_DIMS, preferred_element_type=F32,
+                rt[:, b * RB:(b + 1) * RB, q * BW:(q + 1) * BW].reshape(8 * RB, BW),
+                wout[q // 8, q // 4 % 2, q % 4], NT_DIMS, preferred_element_type=F32,
             )
             part = one if part is None else part + one
         if b in opened:
@@ -344,61 +355,75 @@
     theirs = pl.ds(pl.multiple_of((1 - pc.c) * HH, HH), HH)
     wc, wa, wb, wz, wo = ({} for _ in range(5))
 
-    def do_w2(k):
-        b = k % 2
-        if k >= 2:
-            copy.leave([wc[k - 2]] + wa[k - 2] + wb[k - 2])
-
-        def tile(y, _):
-            cols = pl.ds(pl.multiple_of(k * 4 * BW + y * BW, BW), BW)
-            w2[b, y] = dot(act_t[...], rt[:, :, cols].reshape(ROWS, BW)).astype(BF)
-            return 0
-
-        lax.fori_loop(0, 4, tile, 0)
-        wc[k] = copy(w2.at[b, :, theirs], cr2.at[k], pc.CO)
-
-    def do_w2a(k):
-        b, y = k % 2, pc.ys(2)
-        wc[k].wait_recv()
-        w2[b, y, mine] = w2[b, y, mine] + cr2[k, y]
-        wa[k] = []
-        for d, to in enumerate((pc.YP, pc.YM)):
-            rows = pl.ds(pl.multiple_of(pc.c * HH + d * HH // 2, HH // 2), HH // 2)
-            wa[k].append(copy(w2.at[b, y, rows], ya2.at[k, d], to))
-
-    def do_w2b(k):
-        b = k % 2
-        wb[k] = []
+    def part_rows(d):
+        return pl.ds(pl.multiple_of(pc.c * HH + d * HH // 2, HH // 2), HH // 2)
+
+    def do_w2(w):
+        b, (u, n) = w % 2, W2_UNITS[w]
+        if w >= 2:
+            copy.leave([wc[w - 2]] + wa[w - 2] + wb[w - 2])
+        for i in range(n):
+            for y in (0, 2):
+                lo_col = (u + i) * CW + y * UW
+                part = dot(act_t[...], rt[:, :, lo_col:lo_col + BW].reshape(ROWS, BW)).astype(BF)
+                w2[b, i, y] = part[:, 0:UW]
+                w2[b, i, y + 1] = part[:, UW:BW]
+        wc[w] = copy(w2.at[b, pl.ds(0, n), :, theirs], cr2.at[pl.ds(u, n)], pc.CO)
+
+    def do_w2a(w):
+        b, (u, n), y = w % 2, W2_UNITS[w], pc.ys(2)
+        wc[w].wait_recv()
+        for i in range(n):
+            w2[b, i, y, mine] = w2[b, i, y, mine] + cr2[u + i, y]
+        wa[w] = [
+            copy(w2.at[b, pl.ds(0, n), y, part_rows(d)], ya2.at[d, pl.ds(u, n)], to)
+            for d, to in enumerate((pc.YP, pc.YM))
+        ]
+
+    def do_w2b(w):
+        b, (u, n) = w % 2, W2_UNITS[w]
+        wb[w] = []
         for d, (r, to) in enumerate(((1, pc.YP), (3, pc.YM))):
             y = pc.ys(r)
-            w2[b, y, mine] = w2[b, y, mine] + cr2[k, y]
-            wa[k][d].wait_recv()
-            rows = pl.ds(pl.multiple_of(pc.c * HH + d * HH // 2, HH // 2), HH // 2)
-            w2[b, y, rows] = w2[b, y, rows] + ya2[k, d]
-            wb[k].append(copy(w2.at[b, y, mine], yb2.at[k, d], to))
-
-    def do_w2c(k):
-        for cp in wb[k]:
+            wa[w][d].wait_recv()
+            for i in range(n):
+                w2[b, i, y, mine] = w2[b, i, y, mine] + cr2[u + i, y]
+                w2[b, i, y, part_rows(d)] = w2[b, i, y, part_rows(d)] + ya2[d, u + i]
+            wb[w].append(copy(w2.at[b, pl.ds(0, n), y, mine], yb2.at[d, pl.ds(u, n)], to))
+
+    def do_w2c(w):
+        b, (u, n) = w % 2, W2_UNITS[w]
+        for cp in wb[w]:
             cp.wait_recv()
-        ss[k] = (
-            w2[k % 2, pc.y, mine].astype(F32) + cr2[k, pc.y].astype(F32)
-            + yb2[k, 0].astype(F32) + yb2[k, 1].astype(F32)
-        ).astype(BF)
+        for i in range(n):
+            ss[u + i] = (
+                w2[b, i, pc.y, mine].astype(F32) + cr2[u + i, pc.y].astype(F32)
+                + yb2[0, u + i].astype(F32) + yb2[1, u + i].astype(F32)
+            ).astype(BF)
+
+    z_parts = ((0, 0, 2), (1, 0, 1), (1, 1, 1))
+
+    def unit(z, c, half=0):
+        return (z + 2 * c) * 2 + half
 
     def do_w2z(q):
-        wz[q] = copy(ss.at[1 - pc.zl + 2 * q], zr2.at[q], pc.ZL)
+        c, half, n = z_parts[q]
+        wz[q] = copy(ss.at[pl.ds(unit(1 - pc.zl, c, half), n)], zr2.at[c, pl.ds(half, n)], pc.ZL)
 
     def do_w2s(q):
+        c, half, n = z_parts[q]
         wz[q].wait_recv()
-        ss[pc.zl + 2 * q] = ss[pc.zl + 2 * q] + zr2[q]
+        for h in range(half, half + n):
+            ss[unit(pc.zl, c, h)] = ss[unit(pc.zl, c, h)] + zr2[c, h]
 
     def do_w2o(_):
-        wo[0] = copy(ss.at[pc.zl + 2 * (1 - pc.c)], o2, pc.CO)
+        wo[0] = copy(ss.at[pl.ds(unit(pc.zl, 1 - pc.c), 2)], o2, pc.CO)
 
     def do_w2f(_):
         wo[0].wait_recv()
-        gw2_ref[mine, :] = ss[pc.zl + 2 * pc.c]
-        gw2_ref[theirs, :] = o2[...]
+        for h in range(2):
+            gw2_ref[mine, h * UW:(h + 1) * UW] = ss[unit(pc.zl, pc.c, h)]
+            gw2_ref[theirs, h * UW:(h + 1) * UW] = o2[h]
 
     gx, ga, gb, wi = {}, {}, {}, {}
 
@@ -481,8 +506,8 @@
             (t - jnp.mean(t, axis=1, keepdims=True) - xhat * jnp.mean(t * xhat, axis=1, keepdims=True)) * inv
         ).astype(BF)
 
-    vc, va, vb, vz, ve, vf, vg = {}, {}, {}, {}, [], [], []
-    col_a, col_b = (pl.ds(0, 128), pl.ds(128, 128)), pl.ds(256, 128)
+    vc, va, vb, vz, ve, vf, vg = {}, {}, {}, {}, {}, [], []
+    col_a, col_b = [pl.ds(p * 128, 128) for p in range(CA // 128)], pl.ds(CA, HID - CA)
 
     def w1(z, y, cols, row=0, rows=320):
         return wout.at[pc.c, z, y, pl.ds(row, rows), cols]
@@ -542,18 +567,18 @@
         vz[p].wait_recv()
         gw1_ref[:, p * 128:(p + 1) * 128] = (total_a(p, pc.zl) + zr1[p].astype(F32)).astype(BF)
 
-    def do_e1(_):
-        ve.append(copy(w1(1 - pc.zl, slice(None), col_b), eb1, pc.ZL))
-
-    def do_e2(_):
-        ve[0].wait_recv()
-        for k in (2, 1, 3, 0):
-            y = pc.ys(k)
-            part = w1(pc.zl, y, col_b)
-            part[...] = part[...] + eb1[y]
-            if k == 2:
-                for d, to in enumerate((pc.YP, pc.YM)):
-                    vf.append(copy(w1(pc.zl, y, col_b, d * 160, 160), ec1.at[d], to))
+    def do_e1(k):
+        y = pc.ys(k)
+        ve[k] = copy(w1(1 - pc.zl, y, col_b), eb1.at[y], pc.ZL)
+
+    def do_e2(k):
+        y = pc.ys(k)
+        ve[k].wait_recv()
+        part = w1(pc.zl, y, col_b)
+        part[...] = part[...] + eb1[y]
+        if k == 2:
+            for d, to in enumerate((pc.YP, pc.YM)):
+                vf.append(copy(w1(pc.zl, y, col_b, d * 160, 160), ec1.at[d], to))
 
     def do_e3(_):
         for d, (r, to) in enumerate(((1, pc.YP), (3, pc.YM))):
@@ -566,7 +591,7 @@
     def do_e4(_):
         for cp in vg:
             cp.wait_recv()
-        gw1_ref[:, 256:384] = (
+        gw1_ref[:, CA:HID] = (
             w1(pc.zl, pc.y, col_b)[...].astype(F32) + ed1[0].astype(F32) + ed1[1].astype(F32)
         ).astype(BF)
 
@@ -618,25 +643,25 @@
             buf(HID, ROWS),
             buf(4, 2, SLOTS, HID),
             buf(4, SLOTS, HID),
-            buf(2, 4, HID, BW),
-            buf(4, 4, HH, BW),
-            buf(4, 2, HH // 2, BW),
-            buf(4, 2, HH, BW),
-            buf(4, HH, BW),
-            buf(2, HH, BW),
-            buf(HH, BW),
+            buf(2, 2, 4, HID, UW),
+            buf(8, 4, HH, UW),
+            buf(2, 8, HH // 2, UW),
+            buf(2, 8, HH, UW),
+            buf(8, HH, UW),
+            buf(2, 2, HH, UW),
+            buf(2, HH, UW),
             buf(2, SLOTS, MW // 2),
             buf(2, SLOTS, MW),
             buf(2, 4, 320, HID),
-            buf(2, 2, 2, 160, 128),
-            buf(2, 2, 2, 320, 128),
-            buf(2, 320, 128),
-            buf(4, 320, 128),
-            buf(2, 160, 128),
-            buf(2, 320, 128),
+            buf(CA // 128, 2, 2, 160, 128),
+            buf(CA // 128, 2, 2, 320, 128),
+            buf(CA // 128, 320, 128),
+            buf(4, 320, HID - CA),
+            buf(2, 160, HID - CA),
+            buf(2, 320, HID - CA),
             pltpu.SemaphoreType.DMA((MAX_COPIES,)),
             pltpu.SemaphoreType.DMA((MAX_COPIES,)),
-            pltpu.SemaphoreType.DMA((40,)),
+            pltpu.SemaphoreType.DMA((72,)),
         ],
         compiler_params=pltpu.CompilerParams(
             collective_id=0, has_side_effects=True, vmem_limit_bytes=63 * 2**20
@@ -648,18 +673,32 @@
     )(cnt, own, st, gain, bias, gs, feat, win, wout)
 
 
-def finish_kernel(a, b, c, ao, bo, co):
-    for i, o in ((a, ao), (b, bo), (c, co)):
-        o[...] = i[...]
+def finish_kernel(a, b, c, ao, bo, co, av, bv, cv, sem):
+    ways = [
+        (src.at[rows], mid.at[rows], dst.at[rows])
+        for src, mid, dst, rows in (
+            (a, av, ao, pl.ds(0, 32)), (c, cv, co, pl.ds(0, 384)), (b, bv, bo, pl.ds(0, 320)), (a, av, ao, pl.ds(32, 32))
+        )
+    ]
+    ins = [pltpu.make_async_copy(src, mid, sem.at[n]) for n, (src, mid, _) in enumerate(ways)]
+    outs = [pltpu.make_async_copy(mid, dst, sem.at[n + 4]) for n, (_, mid, dst) in enumerate(ways)]
+    for cp in ins:
+        cp.start()
+    for cp, out in zip(ins, outs):
+        cp.wait()
+        out.start()
+    for out in outs:
+        out.wait()
 
 
 def finish_call(*arrays):
-    vm = pl.BlockSpec(memory_space=pltpu.VMEM)
+    hb = pl.BlockSpec(memory_space=pl.ANY)
     return pl.pallas_call(
         finish_kernel,
         out_shape=tuple(jax.ShapeDtypeStruct(a.shape, a.dtype) for a in arrays),
-        in_specs=[vm] * 3,
-        out_specs=(vm, vm, vm),
+        in_specs=[hb] * 3,
+        out_specs=(hb, hb, hb),
+        scratch_shapes=[pltpu.VMEM(a.shape, a.dtype) for a in arrays] + [pltpu.SemaphoreType.DMA((8,))],
         compiler_params=pltpu.CompilerParams(vmem_limit_bytes=63 * 2**20),
         name="write_results",
     )(*arrays)

time: 138 us -> 137 us (level)
  no operation moved by 1% of the time
where the time goes in v5:
time: 137 us
  Pallas kernels  136 us (99%)
    pallas_call x1, Pallas kernels, merger_call(): pl.pallas_call(merger_kernel, out_shape=(jax.ShapeDtypeStruct((SLOTS, MW)...  134 us

profile of v5, /device:TPU:1, one launch (start us, length us, event | category | flops | bytes accessed | tf_op | source)
XLA Modules:
  0.0 136.5 jit_solution(559077287907299580)
XLA Ops:
  0.6 133.6 %merger_backward.1 = (bf16[64,5120]{1,0:T(8,128)(2,1)}, bf16[320,384]{1,0:T(8,128)(2,1)}, bf16[384,512]{1,0:T(8,128)(2,1)}) custom-call(s32[1,64]{1,0:T(1,128)} %cnt_ref.1, s32[1,64]{1,0:T(1,128)} %own_ref.1, s32[1,64]{1,0:T(1,128)} %st_ref.1, f32[1280]{0:T(1024)} %gain_ref.1, f32[384]{0:T(512)} %b_ref.1, bf16[2,2,64,8192]{3,2,1,0:T(8,128)(2,1)} %bitcast.3, ...), custom_call_target="tpu_custom_call" | custom-call | flops 12482248704 | bytes 16777216 | tf_op jit(solution)/shard_map/merger_backward/pallas_call | solution.py:619
  134.2 2.1 %write_results.1 = (bf16[64,5120]{1,0:T(8,128)(2,1)}, bf16[320,384]{1,0:T(8,128)(2,1)}, bf16[384,512]{1,0:T(8,128)(2,1)}) custom-call(bf16[64,5120]{1,0:T(8,128)(2,1)} %get-tuple-element.9.a, bf16[320,384]{1,0:T(8,128)(2,1)} %get-tuple-element.10.b, bf16[384,512]{1,0:T(8,128)(2,1)} %get-tuple-element.11.c), custom_call_target="tpu_custom_call" | custom-call | tf_op jit(solution)/shard_map/write_results/pallas_call | solution.py:696

commit v6 on v5

--- a/solution.py
+++ b/solution.py
@@ -237,21 +237,25 @@
         return pl.ds(((p // 8) % 2 * 8 + p % 4 * 2 + p // 16) * BW + (p // 4) % 2 * UW, UW)
 
     pc.greet()
-    lf = load(feat_hbm, feat)
+    lf = [load(feat_hbm.at[:, pl.ds(n * VW, VW)], feat.at[:, pl.ds(n * VW, VW)]) for n in range(4)]
     lg = [load(gs_hbm.at[:, :, :, piece(p)], big.at[0:2, :, :, pl.ds(p * UW, UW)]) for p in range(32)]
     gain = gain_ref[...].reshape(1, VW)
-    pack_m[...], route_m[...] = routing_tables(pc, cnt_ref[...], own_ref[...], st_ref[...])
-    lf.wait()
-    lw = load(win_hbm, win)
-    lo = [
-        load(wout_hbm.at[:, piece(p)], wout.at[p // 16, p // 8 % 2, p // 2 % 4, :, pl.ds(p % 2 * UW, UW)])
-        for p in range(32)
-    ]
-    pc.meet()
+    lw, lo = [], []
+
+    def load_weights():
+        lw.append(load(win_hbm, win))
+        for p in range(32):
+            to = wout.at[p // 16, p // 8 % 2, p // 2 % 4, :, pl.ds(p % 2 * UW, UW)]
+            lo.append(load(wout_hbm.at[:, piece(p)], to))
+
+    routed = []
 
     yp, ym, rp, rm, co, zl = ({} for _ in range(6))
 
     def do_pack(i):
+        if not routed:
+            pack_m[...], route_m[...] = routing_tables(pc, cnt_ref[...], own_ref[...], st_ref[...])
+            routed.append(i)
         for p in range(4 * i, 4 * i + 4):
             lg[p].wait()
         g[pc.y, :, cut(i)] = dot(pack_m[...], big[0:2, :, :, cut(i)].reshape(TOK, CW)).astype(BF)
@@ -299,12 +303,17 @@
         return d * inv, inv
 
     def do_norm(n):
+        lf[n].wait()
         nt[me, :, n * VW:(n + 1) * VW] = (standardized(n)[0] * gain).astype(BF)
+        if n == 0:
+            pc.meet()
         ns[n].s1()
+        if n == 0:
+            load_weights()
 
     def do_pre(n):
         if not started:
-            lw.wait()
+            lw[0].wait()
         part = dot(
             nt[:, :, n * VW:(n + 1) * VW].reshape(ROWS, VW), win[n * VW:(n + 1) * VW, :]
         ).reshape(8, SLOTS, HID)

time: 137 us -> 136 us (level)
  no operation moved by 1% of the time
where the time goes in v6:
time: 136 us
  Pallas kernels  135 us (99%)
    pallas_call x1, Pallas kernels, merger_call(): pl.pallas_call(merger_kernel, out_shape=(jax.ShapeDtypeStruct((SLOTS, MW)...  133 us

profile of v6, /device:TPU:1, one launch (start us, length us, event | category | flops | bytes accessed | tf_op | source)
XLA Modules:
  0.0 136.3 jit_solution(15574241863026517154)
XLA Ops:
  0.6 133.4 %merger_backward.1 = (bf16[64,5120]{1,0:T(8,128)(2,1)}, bf16[320,384]{1,0:T(8,128)(2,1)}, bf16[384,512]{1,0:T(8,128)(2,1)}) custom-call(s32[1,64]{1,0:T(1,128)} %cnt_ref.1, s32[1,64]{1,0:T(1,128)} %own_ref.1, s32[1,64]{1,0:T(1,128)} %st_ref.1, f32[1280]{0:T(1024)} %gain_ref.1, f32[384]{0:T(512)} %b_ref.1, bf16[2,2,64,8192]{3,2,1,0:T(8,128)(2,1)} %bitcast.3, ...), custom_call_target="tpu_custom_call" | custom-call | flops 12482248704 | bytes 16777216 | tf_op jit(solution)/shard_map/merger_backward/pallas_call | solution.py:628
  134.0 2.1 %write_results.1 = (bf16[64,5120]{1,0:T(8,128)(2,1)}, bf16[320,384]{1,0:T(8,128)(2,1)}, bf16[384,512]{1,0:T(8,128)(2,1)}) custom-call(bf16[64,5120]{1,0:T(8,128)(2,1)} %get-tuple-element.9.a, bf16[320,384]{1,0:T(8,128)(2,1)} %get-tuple-element.10.b, bf16[384,512]{1,0:T(8,128)(2,1)} %get-tuple-element.11.c), custom_call_target="tpu_custom_call" | custom-call | tf_op jit(solution)/shard_map/write_results/pallas_call | solution.py:705

commit v7 on v6

--- a/solution.py
+++ b/solution.py
@@ -215,7 +215,7 @@
 
 def merger_kernel(
     cnt_ref, own_ref, st_ref, gain_ref, b_ref, gs_hbm, feat_hbm, win_hbm, wout_hbm,
-    mig_ref, gw1_ref, gw2_ref,
+    mig_hbm, gw1_hbm, gw2_hbm, mig_ref, gw1_ref, gw2_ref,
     pack_m, route_m, big, feat, win, win2, wout, g, hc, hz, rt, nt, pre, gh, act_t, gp, gp2,
     w2, cr2, ya2, yb2, ss, zr2, o2, xa, xb, cr1, ya1, yb1, zr1, eb1, ec1, ed1,
     send, recv, lsem,
@@ -248,7 +248,7 @@
             to = wout.at[p // 16, p // 8 % 2, p // 2 % 4, :, pl.ds(p % 2 * UW, UW)]
             lo.append(load(wout_hbm.at[:, piece(p)], to))
 
-    routed = []
+    routed, results = [], []
 
     yp, ym, rp, rm, co, zl = ({} for _ in range(6))
 
@@ -433,6 +433,7 @@
         for h in range(2):
             gw2_ref[mine, h * UW:(h + 1) * UW] = ss[unit(pc.zl, pc.c, h)]
             gw2_ref[theirs, h * UW:(h + 1) * UW] = o2[h]
+        results.append(load(gw2_ref, gw2_hbm))
 
     gx, ga, gb, wi = {}, {}, {}, {}
 
@@ -514,6 +515,7 @@
         mig_ref[rows, at] = (
             (t - jnp.mean(t, axis=1, keepdims=True) - xhat * jnp.mean(t * xhat, axis=1, keepdims=True)) * inv
         ).astype(BF)
+        results.append(load(mig_ref.at[rows, at], mig_hbm.at[rows, at]))
 
     vc, va, vb, vz, ve, vf, vg = {}, {}, {}, {}, {}, [], []
     col_a, col_b = [pl.ds(p * 128, 128) for p in range(CA // 128)], pl.ds(CA, HID - CA)
@@ -575,6 +577,8 @@
     def do_f4(p):
         vz[p].wait_recv()
         gw1_ref[:, p * 128:(p + 1) * 128] = (total_a(p, pc.zl) + zr1[p].astype(F32)).astype(BF)
+        cols = pl.ds(p * 128, 128)
+        results.append(load(gw1_ref.at[:, cols], gw1_hbm.at[:, cols]))
 
     def do_e1(k):
         y = pc.ys(k)
@@ -603,6 +607,7 @@
         gw1_ref[:, CA:HID] = (
             w1(pc.zl, pc.y, col_b)[...].astype(F32) + ed1[0].astype(F32) + ed1[1].astype(F32)
         ).astype(BF)
+        results.append(load(gw1_ref.at[:, col_b], gw1_hbm.at[:, col_b]))
 
     stages = {
         "pack": do_pack, "ring": do_ring, "route": do_route, "across": do_across, "arrive": do_arrive,
@@ -618,6 +623,8 @@
     for name, i in ORDER:
         stages[name](i)
     copy.finish()
+    for cp in results:
+        cp.wait()
     assert len(copy.all) <= MAX_COPIES
 
 
@@ -633,8 +640,11 @@
             jax.ShapeDtypeStruct((HID, BW), BF),
         ),
         in_specs=[vm, vm, vm, vm, vm, hb, hb, hb, hb],
-        out_specs=(vm, vm, vm),
+        out_specs=(hb, hb, hb),
         scratch_shapes=[
+            buf(SLOTS, MW),
+            buf(320, HID),
+            buf(HID, BW),
             buf(SLOTS, TOK),
             buf(4 * SLOTS, 4 * SLOTS),
             buf(4, 2, SLOTS, D),
@@ -670,7 +680,7 @@
             buf(2, 320, HID - CA),
             pltpu.SemaphoreType.DMA((MAX_COPIES,)),
             pltpu.SemaphoreType.DMA((MAX_COPIES,)),
-            pltpu.SemaphoreType.DMA((72,)),
+            pltpu.SemaphoreType.DMA((88,)),
         ],
         compiler_params=pltpu.CompilerParams(
             collective_id=0, has_side_effects=True, vmem_limit_bytes=63 * 2**20

time: 136 us -> 136 us (level)
  no operation moved by 1% of the time
where the time goes in v7:
time: 136 us
  Pallas kernels  135 us (99%)
    pallas_call x1, Pallas kernels, merger_call(): pl.pallas_call(merger_kernel, out_shape=(jax.ShapeDtypeStruct((SLOTS, MW)...  133 us

profile of v7, /device:TPU:1, one launch (start us, length us, event | category | flops | bytes accessed | tf_op | source)
XLA Modules:
  0.0 135.8 jit_solution(5312155763212324400)
XLA Ops:
  0.6 132.8 %merger_backward.1 = (bf16[64,5120]{1,0:T(8,128)(2,1)}, bf16[320,384]{1,0:T(8,128)(2,1)}, bf16[384,512]{1,0:T(8,128)(2,1)}) custom-call(s32[1,64]{1,0:T(1,128)} %cnt_ref.1, s32[1,64]{1,0:T(1,128)} %own_ref.1, s32[1,64]{1,0:T(1,128)} %st_ref.1, f32[1280]{0:T(1024)} %gain_ref.1, f32[384]{0:T(512)} %b_ref.1, bf16[2,2,64,8192]{3,2,1,0:T(8,128)(2,1)} %bitcast.3, ...), custom_call_target="tpu_custom_call" | custom-call | flops 12482248704 | bytes 16777216 | tf_op jit(solution)/shard_map/merger_backward/pallas_call | solution.py:635
  133.5 2.1 %write_results.1 = (bf16[64,5120]{1,0:T(8,128)(2,1)}, bf16[320,384]{1,0:T(8,128)(2,1)}, bf16[384,512]{1,0:T(8,128)(2,1)}) custom-call(bf16[64,5120]{1,0:T(8,128)(2,1)} %get-tuple-element.9.a, bf16[320,384]{1,0:T(8,128)(2,1)} %get-tuple-element.10.b, bf16[384,512]{1,0:T(8,128)(2,1)} %get-tuple-element.11.c), custom_call_target="tpu_custom_call" | custom-call | tf_op jit(solution)/shard_map/write_results/pallas_call | solution.py:715
